TPU v7x, 512 devices: a whole 4x4x16 slice. The times are simulated.
512 devices in a mesh: expert: 8 (over x, core), tensor: 64 (over y, z).
Axes of the slice: x: 4, y: 4, z: 16, core: 2. Of those that a mesh axis runs over, the one named last changes fastest.
Arguments:
- tokens: bfloat16 [256, 6144], P('expert', 'tensor'), may hold values from -6 to 6
- upstream: bfloat16 [256, 6144], P('expert', 'tensor'), may hold values from -3 to 3
- expert_ids: int32 [256, 2], P('expert'), may hold values from 0 to 7, as said below
- slot_pos: int32 [256, 2], P('expert'), may hold values from 0 to 20, as said below
- combine: float32 [256, 2], P('expert'), may hold values from 0.1 to 1
- gate_weight: bfloat16 [8, 6144, 8192], P('expert', None, 'tensor'), may hold values from -0.078125 to 0.078125
- upward_weight: bfloat16 [8, 6144, 8192], P('expert', None, 'tensor'), may hold values from -0.078125 to 0.078125
- down_weight: bfloat16 [8, 8192, 6144], P('expert', 'tensor'), may hold values from -0.0625 to 0.0625
- gate_adapter_first: bfloat16 [8, 6144, 16], P('expert', 'tensor'), may hold values from -0.078125 to 0.078125
- gate_adapter_second: bfloat16 [8, 16, 8192], P('expert', None, 'tensor'), may hold values from -0.29882812 to 0.29882812
- upward_adapter_first: bfloat16 [8, 6144, 16], P('expert', 'tensor'), may hold values from -0.078125 to 0.078125
- upward_adapter_second: bfloat16 [8, 16, 8192], P('expert', None, 'tensor'), may hold values from -0.29882812 to 0.29882812
- down_adapter_first: bfloat16 [8, 8192, 16], P('expert', 'tensor'), may hold values from -0.0625 to 0.0625
- down_right: bfloat16 [8, 16, 6144], P('expert', None, 'tensor'), may hold values from -0.29882812 to 0.29882812
Outputs:
- token_grads: bfloat16 [256, 6144], P('expert', 'tensor')
- combine_grads: float32 [256, 2], P('expert')
- gate_first_gradient: float32 [8, 6144, 16], P('expert', 'tensor')
- gate_second_gradient: float32 [8, 16, 8192], P('expert', None, 'tensor')
- upward_first_gradient: float32 [8, 6144, 16], P('expert', 'tensor')
- upward_second_gradient: float32 [8, 16, 8192], P('expert', None, 'tensor')
- down_first_gradient: float32 [8, 8192, 16], P('expert', 'tensor')
- down_second_gradient: float32 [8, 16, 6144], P('expert', None, 'tensor')
Inputs may be any that keep to these rules, and one draw needn't show every extreme that they name: `expert_ids`: each token names two different experts. Within each block of 32 consecutive tokens no expert is named by more than 21 tokens, one expert by exactly 21, and every expert by at least one. `slot_pos`: A token's slot for an expert is the number of earlier tokens of its block that name the same expert, so slots of one block and expert are 0, 1, 2 and so on without gaps.
All inputs are finite; a program needn't handle non-finite values.
Results may differ from a plain program's by a relative error of at most 0.024.
Values may be sent and summed in bfloat16 or wider, within the bound.
A program may use at most 64 MiB of HBM per device.

v0:
```python
import jax
import jax.numpy as jnp
from jax import lax
from jax.sharding import PartitionSpec as P

CAP = 21


adapter_scale_factor = 2.0


def silu_terms(gate_preactivation):
    sigmoid = jax.nn.sigmoid(gate_preactivation)
    active = gate_preactivation * sigmoid
    slope = sigmoid * (1.0 + gate_preactivation * (1.0 - sigmoid))
    return (active, slope)


def local(
    tokens,
    upstream,
    expert_ids,
    slot_pos,
    combine,
    gate_weight,
    upward_weight,
    down_weight,
    gate_adapter_first,
    gate_adapter_second,
    upward_adapter_first,
    upward_adapter_second,
    down_adapter_first,
    down_right,
):
    groups = lax.axis_size("expert")
    local_experts = gate_weight.shape[0]
    experts_all = local_experts * groups
    width_loc = tokens.shape[1]
    capacity = CAP
    f32 = jnp.float32
    bf16 = jnp.bfloat16
    highest = lax.Precision.HIGHEST
    columns = expert_ids * capacity + slot_pos
    column_iota = jnp.arange(experts_all * capacity, dtype=jnp.int32)
    pick_first = (columns[:, 0:1] == column_iota[None, :]).astype(f32)
    pick_second = (columns[:, 1:2] == column_iota[None, :]).astype(f32)
    pick_sum = pick_first + pick_second
    pick_both = pick_sum.astype(bf16)
    slot_combine = jnp.sum(
        pick_first * combine[:, 0:1] + pick_second * combine[:, 1:2], axis=0
    ).reshape(experts_all, capacity)

    def to_slots(row_data):
        placed = lax.dot_general(
            pick_both, row_data, (((0,), (0,)), ((), ())), preferred_element_type=f32
        )
        return placed.astype(bf16).reshape(experts_all, capacity, row_data.shape[1])

    local_x, local_dy, slot_weight = (
        lax.all_to_all(to_slots(tokens), "expert", split_axis=0, concat_axis=1, tiled=True),
        lax.all_to_all(to_slots(upstream), "expert", split_axis=0, concat_axis=1, tiled=True),
        lax.all_to_all(
            slot_combine.astype(jnp.bfloat16), "expert", split_axis=0, concat_axis=1, tiled=True
        ).astype(slot_combine.dtype),
    )
    x_piece = lax.all_gather(local_x, "tensor", axis=2, tiled=True)
    dy_piece = lax.all_gather(local_dy, "tensor", axis=2, tiled=True)
    gate_rows = gate_weight
    lift_rows = upward_weight
    gate_preactivation = jnp.einsum("esc,ecf->esf", x_piece, gate_rows, preferred_element_type=f32)
    upward_preactivation = jnp.einsum(
        "esc,ecf->esf", x_piece, lift_rows, preferred_element_type=f32
    )
    hidden_backward = jnp.einsum("esc,efc->esf", dy_piece, down_weight, preferred_element_type=f32)
    totals = (gate_preactivation, upward_preactivation, hidden_backward)
    gate_preactivation, upward_preactivation, hidden_backward = totals
    gate_reduced, upward_reduced, down_reduced = lax.psum(
        (
            jnp.einsum("esc,ecr->esr", local_x, gate_adapter_first, preferred_element_type=f32),
            jnp.einsum("esc,ecr->esr", local_x, upward_adapter_first, preferred_element_type=f32),
            jnp.einsum("esc,erc->esr", local_dy, down_right, preferred_element_type=f32),
        ),
        "tensor",
    )
    gate_lowb = gate_reduced.astype(bf16)
    lift_lowb = upward_reduced.astype(bf16)
    down_lowb = down_reduced.astype(bf16)
    gate_preactivation = gate_preactivation + adapter_scale_factor * jnp.einsum(
        "esr,erf->esf", gate_lowb, gate_adapter_second, preferred_element_type=f32
    )
    upward_preactivation = upward_preactivation + adapter_scale_factor * jnp.einsum(
        "esr,erf->esf", lift_lowb, upward_adapter_second, preferred_element_type=f32
    )
    active, slope = silu_terms(gate_preactivation)
    hidden_state = (active * upward_preactivation).astype(bf16)
    hidden_backward = hidden_backward + adapter_scale_factor * jnp.einsum(
        "esr,efr->esf", down_lowb, down_adapter_first, preferred_element_type=f32
    )
    weight_col = slot_weight[:, :, None]
    grad_hidden = weight_col * hidden_backward
    gate_gradient = (grad_hidden * upward_preactivation * slope).astype(bf16)
    upward_gradient = (grad_hidden * active).astype(bf16)
    partial_combine = jnp.sum(hidden_state.astype(f32) * hidden_backward, axis=2)
    hidden_low = jnp.einsum(
        "esf,efr->esr", hidden_state, down_adapter_first, preferred_element_type=f32
    )
    gate_backward = jnp.einsum(
        "esf,erf->esr", gate_gradient, gate_adapter_second, preferred_element_type=f32
    )
    upward_backward = jnp.einsum(
        "esf,erf->esr", upward_gradient, upward_adapter_second, preferred_element_type=f32
    )
    hidden_low, gate_backward, upward_backward, slot_grads = lax.psum(
        (hidden_low, gate_backward, upward_backward, partial_combine), "tensor"
    )
    reduced_weighted = (weight_col * hidden_low).astype(bf16)
    down_weighted = (weight_col * down_reduced).astype(bf16)
    gate_backb = gate_backward.astype(bf16)
    lift_backb = upward_backward.astype(bf16)
    down_second_gradient = adapter_scale_factor * jnp.einsum(
        "esr,esc->erc", reduced_weighted, local_dy, preferred_element_type=f32
    )
    down_first_gradient = adapter_scale_factor * jnp.einsum(
        "esf,esr->efr", hidden_state, down_weighted, preferred_element_type=f32
    )
    gate_second_gradient = adapter_scale_factor * jnp.einsum(
        "esr,esf->erf", gate_lowb, gate_gradient, preferred_element_type=f32
    )
    upward_second_gradient = adapter_scale_factor * jnp.einsum(
        "esr,esf->erf", lift_lowb, upward_gradient, preferred_element_type=f32
    )
    gate_first_gradient = adapter_scale_factor * jnp.einsum(
        "esc,esr->ecr", local_x, gate_backb, preferred_element_type=f32
    )
    upward_first_gradient = adapter_scale_factor * jnp.einsum(
        "esc,esr->ecr", local_x, lift_backb, preferred_element_type=f32
    )
    reduced_portion = jnp.einsum(
        "ecr,esr->ces", gate_adapter_first, gate_backb, preferred_element_type=f32
    )
    reduced_portion = reduced_portion + jnp.einsum(
        "ecr,esr->ces", upward_adapter_first, lift_backb, preferred_element_type=f32
    )
    grads_comb = slot_grads.reshape(1, local_experts, groups, capacity)
    gate_rows = gate_weight
    lift_rows = upward_weight
    term = jnp.einsum("ecf,esf->ces", gate_rows, gate_gradient, preferred_element_type=f32)
    summed_result = lax.psum_scatter(
        term + jnp.einsum("ecf,esf->ces", lift_rows, upward_gradient, preferred_element_type=f32),
        "tensor",
        scatter_dimension=0,
        tiled=True,
    )
    slot_input_rows = (summed_result + adapter_scale_factor * reduced_portion).reshape(
        width_loc, local_experts, groups, capacity
    )
    returned, returned_comb = (
        lax.all_to_all(
            slot_input_rows.astype(jnp.bfloat16), "expert", split_axis=2, concat_axis=1, tiled=True
        ).astype(slot_input_rows.dtype),
        lax.all_to_all(
            grads_comb.astype(jnp.bfloat16), "expert", split_axis=2, concat_axis=1, tiled=True
        ).astype(grads_comb.dtype),
    )
    returned = returned.reshape(width_loc, experts_all * capacity)
    token_grads = lax.dot_general(
        pick_sum, returned, (((1,), (1,)), ((), ())), precision=highest, preferred_element_type=f32
    ).astype(bf16)
    returned_comb = returned_comb.reshape(1, experts_all * capacity)
    combine_grads = jnp.stack(
        [jnp.sum(pick_first * returned_comb, axis=1), jnp.sum(pick_second * returned_comb, axis=1)],
        axis=1,
    )
    return (
        token_grads,
        combine_grads,
        gate_first_gradient,
        gate_second_gradient,
        upward_first_gradient,
        upward_second_gradient,
        down_first_gradient,
        down_second_gradient,
    )


def solution(mesh):
    in_specs = (
        P("expert", "tensor"),
        P("expert", "tensor"),
        P("expert", None),
        P("expert", None),
        P("expert", None),
        P("expert", None, "tensor"),
        P("expert", None, "tensor"),
        P("expert", "tensor", None),
        P("expert", "tensor", None),
        P("expert", None, "tensor"),
        P("expert", "tensor", None),
        P("expert", None, "tensor"),
        P("expert", "tensor", None),
        P("expert", None, "tensor"),
    )
    out_specs = (
        P("expert", "tensor"),
        P("expert", None),
        P("expert", "tensor", None),
        P("expert", None, "tensor"),
        P("expert", "tensor", None),
        P("expert", None, "tensor"),
        P("expert", "tensor", None),
        P("expert", None, "tensor"),
    )
    return jax.shard_map(local, mesh=mesh, in_specs=in_specs, out_specs=out_specs, check_vma=False)
```

profile of v0, /device:TPU:1, one launch (start us, length us, event | category | flops | bytes accessed | tf_op | source)
XLA Modules:
  0.0 1242.5 jit_solution(7020119511862114615)
XLA Ops:
  9.0 14.0 %all_to_all.52 = bf16[8,21,96]{2,1,0:T(8,128)(2,1)S(1)} all-to-all(bf16[8,21,96]{2,1,0:T(8,128)(2,1)S(1)} %reshape.272), channel_id=1, replica_groups=mesh['expert'=8,'tensor'=64] {'expert'}, dimensions={0} | all-to-all | bytes 64512 | tf_op jit(solution)/shard_map/all_to_all | solution.py:60
  24.0 1.0 convolution_convert_fusion.1
  25.0 7.9 all_to_all.53
  36.3 227.8 %all-reduce.1 = (bf16[1,168,16]{1,2,0:T(8,128)(2,1)S(1)}, bf16[1,168,16]{1,2,0:T(8,128)(2,1)S(1)}, f32[1,168,16]{1,2,0:T(8,128)S(1)}) all-reduce(f32[1,168,16]{1,2,0:T(8,128)S(1)} %convolution_bitcast_fusion.3, f32[1,168,16]{1,2,0:T(8,128)S(1)} %convolution_bitcast_fusion.4, ...), channel_id=1, replica_groups=mesh['expert'=8,'tensor'=64] {'tensor'}, use_global_device_ids=true, to_apply=%region_3.0 | all-reduce | flops 8064 | bytes 53760 | tf_op jit(solution)/shard_map/psum | solution.py:77
  265.0 1.5 convolution_multiply_fusion.1
  267.5 13.3 %copy.37 = bf16[1,168,6144]{2,1,0:T(8,128)(2,1)} copy(bf16[1,168,6144]{1,0,2:T(2,128)(2,1)} %all-gather.5.cloned.1.call-done) | data formatting | bytes 4128768 | tf_op jit(solution)/shard_map/all_gather | solution.py:66
  280.8 2.5 fusion.23
  284.2 33.1 %all-gather.3.cloned.1.call-done = bf16[1,168,6144]{1,0,2:T(2,128)(2,1)} async-done(((bf16[1,168,96]{1,0,2:T(2,128)(2,1)}), bf16[1,168,6144]{1,0,2:T(2,128)(2,1)}) %all-gather.3.cloned.1.call-update) | async-done | bytes 2064400 | tf_op jit(solution)/shard_map/all_gather | solution.py:67
  317.3 13.3 %copy.35 = bf16[1,168,6144]{2,1,0:T(8,128)(2,1)} copy(bf16[1,168,6144]{1,0,2:T(2,128)(2,1)} %all-gather.3.cloned.1.call-done) | data formatting | bytes 4128768 | tf_op jit(solution)/shard_map/all_gather | solution.py:67
  330.6 3.4 multiply_reduce_fusion
  333.9 114.7 %psum.54 = bf16[1,168]{1,0:T(2,128)(2,1)S(1)} all-reduce(f32[1,168]{1,0:T(1,128)S(1)} %bitcast.168), channel_id=1, replica_groups=mesh['expert'=8,'tensor'=64] {'tensor'}, use_global_device_ids=true, to_apply=%region_8.0 | all-reduce | flops 168 | bytes 1008 | tf_op jit(solution)/shard_map/psum | solution.py:113
  449.3 51.7 %all-to-all-start.4 = ((bf16[1,1,8,21]{3,1,0,2:T(2,128)(2,1)}), bf16[1,1,8,21]{3,1,0,2:T(2,128)(2,1)S(1)}, u32[]{:S(2)}, u32[]{:S(2)}) async-start(bf16[1,1,8,21]{3,1,0,2:T(2,128)(2,1)} %convert_element_type.151), calls=%async_computation.4 | async-start | bytes 8192 | tf_op jit(solution)/shard_map/all_to_all | solution.py:161
  501.8 3.8 all-to-all-done.4
  505.7 1.4 select_reduce_fusion.1
  507.1 7.6 all_to_all.54
  514.8 1.0 multiply_convert_fusion.1
  515.8 1.2 fusion.7
  517.0 3.2 fusion
  520.2 6.1 copy.42
  528.0 221.2 %all-reduce = (bf16[1,168,16]{1,2,0:T(8,128)(2,1)S(1)}, bf16[1,168,16]{1,2,0:T(8,128)(2,1)S(1)}, f32[1,168,16]{1,2,0:T(8,128)S(1)}) all-reduce(f32[1,168,16]{1,2,0:T(8,128)S(1)} %convolution_bitcast_fusion.2, f32[1,168,16]{1,2,0:T(8,128)S(1)} %convolution_bitcast_fusion.1, ...), channel_id=1, replica_groups=mesh['expert'=8,'tensor'=64] {'tensor'}, use_global_device_ids=true, to_apply=%region_5.0 | all-reduce | flops 8064 | bytes 53760 | tf_op jit(solution)/shard_map/psum | solution.py:113
  753.1 459.9 %reduce-scatter.4.cloned.1.call-done = f32[96,168]{1,0:T(8,128)} async-done(((f32[6144,168]{1,0:T(8,128)}), f32[96,168]{1,0:T(8,128)}) %reduce-scatter.4.cloned.1.call-update) | async-done | bytes 64528
  1213.0 1.0 copy.43
  1214.8 15.5 %all-to-all-start.3 = ((bf16[96,1,8,21]{0,3,1,2:T(8,128)(2,1)}), bf16[96,1,8,21]{0,3,1,2:T(8,128)(2,1)S(1)}, u32[]{:S(2)}, u32[]{:S(2)}) async-start(bf16[96,1,8,21]{0,3,1,2:T(8,128)(2,1)} %bitcast.29), calls=%async_computation.3 | async-start | bytes 98304 | tf_op jit(solution)/shard_map/all_to_all | solution.py:158
  1231.0 4.1 all-to-all-done.3
  (85 shorter events, 18.5 us)
Async XLA Ops:
  7.2 273.6 %copy-start = (bf16[1,6144,128]{2,1,0:T(8,128)(2,1)S(1)}, bf16[1,6144,128]{2,1,0:T(8,128)(2,1)}, u32[]{:S(2)}) copy-start(bf16[1,6144,128]{2,1,0:T(8,128)(2,1)} %param.19) | copy-start | bytes 4718596
  7.2 260.3 %all-gather.5.cloned.1.call-start = ((), (), s32[]{:S(2)}) async-start(), calls=%async_computation.7 | async-start | bytes 6389760 | tf_op jit(solution)/shard_map/all_gather | solution.py:66
  8.0 15.9 %copy-start.15 = (s32[32]{0:T(128)}, s32[32]{0:T(128)S(1)}, u32[]{:S(2)}) copy-start(s32[32]{0:T(128)S(1)} %get-tuple-element.24) | copy-start | bytes 388
  8.0 497.6 %copy-start.13 = (s32[32]{0:T(128)}, s32[32]{0:T(128)S(1)}, u32[]{:S(2)}) copy-start(s32[32]{0:T(128)S(1)} %get-tuple-element.23) | copy-start | bytes 388
  23.9 293.4 %all-gather.3.cloned.1.call-start = ((), (), s32[]{:S(2)}) async-start(), calls=%async_computation.6 | async-start | bytes 6389760 | tf_op jit(solution)/shard_map/all_gather | solution.py:67
  264.1 3.3 copy-start.4
  264.1 3.4 copy-start.6
  280.8 2.5 copy-start.1
  280.8 2.7 copy-start.2
  280.8 2.7 copy-start.3
  449.3 56.2 %all-to-all-start.4 = ((bf16[1,1,8,21]{3,1,0,2:T(2,128)(2,1)}), bf16[1,1,8,21]{3,1,0,2:T(2,128)(2,1)S(1)}, u32[]{:S(2)}, u32[]{:S(2)}) async-start(bf16[1,1,8,21]{3,1,0,2:T(2,128)(2,1)} %convert_element_type.151), calls=%async_computation.4 | async-start | bytes 8192 | tf_op jit(solution)/shard_map/all_to_all | solution.py:161
  501.0 711.9 %reduce-scatter.4.cloned.1.call-start = ((), (), s32[]{:S(2)}) async-start(), calls=%async_computation.8 | async-start | bytes 6389760
  526.3 0.7 copy-start.12
  526.3 0.8 copy-start.17
  526.3 0.8 copy-start.18
  526.3 1.4 copy-start.9
  526.3 1.6 copy-start.10
  526.3 222.9 %copy-start.7 = (bf16[1,168,16]{1,2,0:T(8,128)(2,1)S(1)}, bf16[1,168,16]{1,2,0:T(8,128)(2,1)}, u32[]{:S(2)}) copy-start(bf16[1,168,16]{1,2,0:T(8,128)(2,1)} %copy-done.6) | copy-start | bytes 16132
  526.3 225.1 %copy-start.5 = (f32[1,168,16]{1,2,0:T(8,128)S(1)}, f32[1,168,16]{1,2,0:T(8,128)}, u32[]{:S(2)}) copy-start(f32[1,168,16]{1,2,0:T(8,128)} %copy-done.4) | copy-start | bytes 32260
  526.3 226.5 %copy-start.11 = (bf16[1,96,16]{1,2,0:T(8,128)(2,1)S(1)}, bf16[1,96,16]{1,2,0:T(8,128)(2,1)}, u32[]{:S(2)}) copy-start(bf16[1,96,16]{1,2,0:T(8,128)(2,1)} %param.22) | copy-start | bytes 9220
  526.4 687.6 %copy-start.8 = (bf16[1,96,16]{1,2,0:T(8,128)(2,1)S(1)}, bf16[1,96,16]{1,2,0:T(8,128)(2,1)}, u32[]{:S(2)}) copy-start(bf16[1,96,16]{1,2,0:T(8,128)(2,1)} %param.24) | copy-start | bytes 9220
  526.4 708.7 %copy-start.14 = (s32[32]{0:T(128)S(1)}, s32[32]{0:T(128)}, u32[]{:S(2)}) copy-start(s32[32]{0:T(128)} %copy-done.13) | copy-start | bytes 388
  526.4 708.7 %copy-start.16 = (s32[32]{0:T(128)S(1)}, s32[32]{0:T(128)}, u32[]{:S(2)}) copy-start(s32[32]{0:T(128)} %copy-done.15) | copy-start | bytes 388
  1214.8 20.3 %all-to-all-start.3 = ((bf16[96,1,8,21]{0,3,1,2:T(8,128)(2,1)}), bf16[96,1,8,21]{0,3,1,2:T(8,128)(2,1)S(1)}, u32[]{:S(2)}, u32[]{:S(2)}) async-start(bf16[96,1,8,21]{0,3,1,2:T(8,128)(2,1)} %bitcast.29), calls=%async_computation.3 | async-start | bytes 98304 | tf_op jit(solution)/shard_map/all_to_all | solution.py:158
Sparse Core Ops, SparseCore 0:
  24.0 143.4 all-gather.4
  170.4 146.8 all-gather.2
  526.5 686.3 reduce-scatter.3
where the time goes:
time: 1240 us
  blocking collectives  593 us (48%)
  waiting for transfers between devices  501 us (40%)
  starting transfers between devices  67.3 us (5%)
  local copies, waits for them, and re-layouts  38.6 us (3%)
  matrix products  24.8 us (2%)
  between operations  14 us (1%)
    unnamed x4, waiting for transfers between devices  460 us
    psum x2, blocking collectives, local(): lax.psum((hidden_low, gate_backward, upward_backward, partial_combine), '...  336 us
    psum x1, blocking collectives, local(): lax.psum((jnp.einsum('esc,ecr->esr', local_x, gate_adapter_first, preferr...  228 us
    all_to_all x1, starting transfers between devices, local(): lax.all_to_all(grads_comb.astype(jnp.bfloat16), 'expert', split_axis=2, c...  51.7 us
    all_gather x1, waiting for transfers between devices, local(): dy_piece = lax.all_gather(local_dy, 'tensor', axis=2, tiled=True)  33.1 us
  transfers between devices with their start and end apart: 5, of which 4 were waited for; matrix products, arithmetic and copies ran while one was open for 2% of the time, Pallas kernels for 0%

commit v1 on v0

v1 whole, which is shorter than its diff:
```python
import jax
import jax.numpy as jnp
from jax import lax
from jax.experimental import pallas as pl
from jax.experimental.pallas import tpu as pltpu
from jax.sharding import PartitionSpec as P

MESH = pl.DeviceIdType.MESH
F32 = jnp.float32
BF16 = jnp.bfloat16
SCALE = 2.0
NX, NY, NZ, NC = 4, 4, 16, 2
TB = 32
FD = 96
HR = 48
HID = 128
NT = 256
STEP = 4 * FD
PAIR = 2


def dot_nn(a, b):
    return lax.dot_general(a, b, (((1,), (0,)), ((), ())), preferred_element_type=F32)


def dot_nt(a, b):
    return lax.dot_general(a, b, (((1,), (1,)), ((), ())), preferred_element_type=F32)


def dot_tn(a, b):
    return lax.dot_general(a, b, (((0,), (0,)), ((), ())), preferred_element_type=F32)


def remote(src, dst, send, recv, dev):
    return pltpu.make_async_remote_copy(
        src_ref=src, dst_ref=dst, send_sem=send, recv_sem=recv, device_id=dev, device_id_type=MESH
    )


def loop(low, high, body):
    def step(i, carry):
        body(i)
        return carry

    lax.fori_loop(low, high, step, 0)


def kernel(
    tok,
    ups,
    ids,
    comb,
    w1_hbm,
    w3_hbm,
    w2_hbm,
    a1t,
    b1,
    a3t,
    b3,
    d1t,
    rj,
    tg,
    cg,
    gft,
    gs,
    uft,
    us,
    dft,
    ds,
    w1,
    w3,
    w2,
    w13t,
    src,
    disp,
    xj,
    gj,
    own,
    gat,
    acch,
    accq,
    et,
    part,
    rsb,
    ysend,
    yrec,
    full,
    yb,
    rc,
    axb,
    byb,
    ya,
    yc,
    ayb,
    bxb,
    zsend,
    zr,
    fscr,
    fsend,
    fin,
    ascr,
    asend,
    afin,
    w_sem,
    d_ss,
    d_rs,
    z_ss,
    z_rs,
    a1_ss,
    a1_rs,
    b1_ss,
    b1_rs,
    a2_ss,
    a2_rs,
    b2_ss,
    b2_rs,
    s1_ss,
    s1_rs,
    s2_ss,
    s2_rs,
    r_ss,
    r_rs,
    y_ss,
    y_rs,
    g_ss,
    g_rs,
    k_ss,
    k_rs,
    p1_ss,
    p1_rs,
    p2_ss,
    p2_rs,
    p3_ss,
    p3_rs,
    f_ss,
    f_rs,
    h_ss,
    h_rs,
):
    e = lax.axis_index("expert")
    j = lax.axis_index("tensor")
    x = e // 2
    c = lax.rem(e, 2)
    y = j // NZ
    z = lax.rem(j, NZ)
    sib = (2 * x + 1 - c, j)

    def at_x(v):
        return (2 * v + c, j)

    def at_y(v):
        return (e, v * NZ + z)

    def at_z(v):
        return (e, y * NZ + v)

    bar = pltpu.get_barrier_semaphore()

    def sig_e(i):
        pl.semaphore_signal(bar, inc=1, device_id=(lax.rem(e + i, 8), j), device_id_type=MESH)

    def sig_z(i):
        pl.semaphore_signal(bar, inc=1, device_id=at_z(lax.rem(z + i, NZ)), device_id_type=MESH)

    def sig_y(i):
        pl.semaphore_signal(bar, inc=1, device_id=at_y(lax.rem(y + i, NY)), device_id_type=MESH)

    loop(1, NZ, sig_z)
    loop(1, NY, sig_y)
    loop(1, 8, sig_e)

    loads = [
        pltpu.make_async_copy(w1_hbm.at[0], w1, w_sem.at[0]),
        pltpu.make_async_copy(w3_hbm.at[0], w3, w_sem.at[1]),
        pltpu.make_async_copy(w2_hbm.at[0], w2, w_sem.at[2]),
    ]
    for load in loads:
        load.start()

    lane = lax.broadcasted_iota(jnp.int32, (TB, 128), 1)
    idv = ids[...]
    cv = comb[...]
    dense = jnp.zeros((TB, 128), F32)
    for k in range(2):
        hit = (lane - FD == idv[:, k : k + 1]) | (lane - FD - 8 == idv[:, k : k + 1])
        dense = dense + jnp.where(hit, cv[:, k : k + 1], 0.0)
    high = dense.astype(BF16)
    low = (dense - high.astype(F32)).astype(BF16)
    src[0:TB, :] = jnp.where(lane < FD + 8, high.astype(F32), low.astype(F32)).astype(BF16)
    src[0:TB, 0:FD] = tok[...]
    src[TB : 2 * TB, :] = jnp.zeros((TB, 128), BF16)
    src[TB : 2 * TB, 0:FD] = ups[...]
    disp[e] = src[...]

    for load in loads:
        load.wait()

    def flip(i):
        rows = pl.ds(pl.multiple_of(i * 128, 128), 128)
        w13t[0:HID, rows] = jnp.transpose(w1[rows, :])
        w13t[HID : 2 * HID, rows] = jnp.transpose(w3[rows, :])

    loop(0, 48, flip)

    pl.semaphore_wait(bar, 7 + NZ - 1 + NY - 1)

    def disp_copy(i, slot):
        return remote(
            src, disp.at[slot], d_ss.at[i], d_rs.at[i], (lax.rem(e + i, 8), j)
        )

    loop(1, 8, lambda i: disp_copy(i, e).start())
    loop(1, 8, lambda i: disp_copy(i, lax.rem(e + 8 - i, 8)).wait())

    xt = jnp.transpose(disp[:, 0:TB, :].reshape(NT, 128))
    gt = jnp.transpose(disp[:, TB : 2 * TB, :].reshape(NT, 128))
    row = lax.broadcasted_iota(jnp.int32, (32, NT), 0)
    tail = xt[FD:128, :].astype(F32)
    weight = jnp.sum(jnp.where((row == e) | (row == e + 8), tail, 0.0), axis=0, keepdims=True)
    xj[...] = xt[0:FD, :]
    gj[...] = gt[0:FD, :]
    for half in range(2):
        for th in range(2):
            cut = slice(128 * th, 128 * th + 128)
            rows = slice(HR * half, HR * half + HR)
            own[th, half] = xt[rows, cut]
            own[2 + th, half] = gt[rows, cut]
    gat[x, y, z, c] = own[x, c]

    def z_copy(i, slot):
        piece = gat.at[x, y, slot, c]
        return remote(piece, piece, z_ss.at[i], z_rs.at[i], at_z(lax.rem(z + i, NZ)))

    loop(1, NZ, lambda i: z_copy(i, z).start())

    def sum_start(n, value):
        for k in range(NZ):
            part[n, k] = value[8 * (k // 2) : 8 * (k // 2) + 8, 128 * (k % 2) : 128 * (k % 2) + 128]
        rsb[n, z] = part[n, z]

        def go(i):
            to = lax.rem(z + i, NZ)
            remote(part.at[n, to], rsb.at[n, z], r_ss.at[n, i], r_rs.at[n, i], at_z(to)).start()

        loop(1, NZ, go)

    def y_copy(n, i, slot):
        return remote(
            ysend.at[n], yrec.at[n, slot], y_ss.at[n, i], y_rs.at[n, i], at_y(lax.rem(y + i, NY))
        )

    def sum_middle(n):
        def done(i):
            to = lax.rem(z + i, NZ)
            remote(
                part.at[n, to],
                rsb.at[n, lax.rem(z + NZ - i, NZ)],
                r_ss.at[n, i],
                r_rs.at[n, i],
                at_z(to),
            ).wait()

        loop(1, NZ, done)
        total = jnp.sum(rsb[n], axis=0)
        ysend[n] = total
        yrec[n, y] = total
        loop(1, NY, lambda i: y_copy(n, i, y).start())

    def g_copy(n, i, slot):
        piece = full.at[n, slot]
        return remote(piece, piece, g_ss.at[n, i], g_rs.at[n, i], at_z(lax.rem(z + i, NZ)))

    def sum_last(n):
        loop(1, NY, lambda i: y_copy(n, i, lax.rem(y + NY - i, NY)).wait())
        full[n, z] = jnp.sum(yrec[n], axis=0)
        loop(1, NZ, lambda i: g_copy(n, i, z).start())

    def sum_done(n):
        loop(1, NZ, lambda i: g_copy(n, i, lax.rem(z + NZ - i, NZ)).wait())
        return jnp.concatenate(
            [jnp.concatenate([full[n, 2 * k], full[n, 2 * k + 1]], axis=1) for k in range(8)], axis=0
        )

    a13t = jnp.concatenate([a1t[0], a3t[0]], axis=0)
    sum_start(
        0,
        jnp.concatenate(
            [dot_nn(a13t, xj[...]), dot_nn(rj[0], gj[...]), jnp.zeros((16, NT), F32)], axis=0
        ),
    )

    loop(1, NZ, lambda i: z_copy(i, lax.rem(z + NZ - i, NZ)).wait())
    sum_middle(0)

    ahead_x = lax.rem(x + 1 + 2 * c, NX)
    behind_x = lax.rem(x + 3 + 2 * c, NX)
    far_x = lax.rem(x + 2, NX)
    ahead_y = lax.rem(y + 1 + 2 * c, NY)
    behind_y = lax.rem(y + 3 + 2 * c, NY)
    far_y = lax.rem(y + 2, NY)

    def a1_copy(k, of, to):
        piece = gat.at[of, y, 0:8, c]
        return remote(piece, piece, a1_ss.at[k], a1_rs.at[k], at_x(to))

    def b1_copy(k, of, to):
        piece = gat.at[x, of, 8:16, c]
        return remote(piece, piece, b1_ss.at[k], b1_rs.at[k], at_y(to))

    a1_copy(0, x, ahead_x).start()
    b1_copy(0, y, ahead_y).start()
    a1_copy(1, x, behind_x).start()
    b1_copy(1, y, behind_y).start()
    a1_copy(0, behind_x, ahead_x).wait_recv()
    a1_copy(2, behind_x, ahead_x).start()
    b1_copy(0, behind_y, ahead_y).wait_recv()
    b1_copy(2, behind_y, ahead_y).start()
    a1_copy(1, ahead_x, behind_x).wait_recv()
    b1_copy(1, ahead_y, behind_y).wait_recv()
    sum_last(0)
    a1_copy(2, far_x, ahead_x).wait_recv()
    b1_copy(2, far_y, ahead_y).wait_recv()

    def a2_copy(k, i, of, to):
        piece = gat.at[:, of, pl.ds(PAIR * i, PAIR), c]
        return remote(piece, piece, a2_ss.at[k, i], a2_rs.at[k, i], at_y(to))

    def b2_copy(k, i, of, to):
        piece = gat.at[of, :, pl.ds(8 + PAIR * i, PAIR), c]
        return remote(piece, piece, b2_ss.at[k, i], b2_rs.at[k, i], at_x(to))

    def sa_copy(k, i, of, core):
        piece = gat.at[:, of, pl.ds(PAIR * i, PAIR), core]
        return remote(piece, piece, s1_ss.at[k, i], s1_rs.at[k, i], sib)

    def sb_copy(k, i, of, core):
        piece = gat.at[of, :, pl.ds(8 + PAIR * i, PAIR), core]
        return remote(piece, piece, s2_ss.at[k, i], s2_rs.at[k, i], sib)

    chunks = 8 // PAIR

    def wide_start(i):
        a2_copy(0, i, y, ahead_y).start()
        b2_copy(0, i, x, ahead_x).start()
        a2_copy(1, i, y, behind_y).start()
        b2_copy(1, i, x, behind_x).start()
        sa_copy(0, i, y, c).start()
        sb_copy(0, i, x, c).start()

    loop(0, chunks, wide_start)

    def wide_pass(i):
        a2_copy(0, i, behind_y, ahead_y).wait_recv()
        a2_copy(2, i, behind_y, ahead_y).start()
        sa_copy(1, i, behind_y, c).start()
        b2_copy(0, i, behind_x, ahead_x).wait_recv()
        b2_copy(2, i, behind_x, ahead_x).start()
        sb_copy(1, i, behind_x, c).start()
        a2_copy(1, i, ahead_y, behind_y).wait_recv()
        sa_copy(2, i, ahead_y, c).start()
        b2_copy(1, i, ahead_x, behind_x).wait_recv()
        sb_copy(2, i, ahead_x, c).start()

    loop(0, chunks, wide_pass)

    def wide_end(i):
        a2_copy(2, i, far_y, ahead_y).wait_recv()
        sa_copy(3, i, far_y, c).start()
        b2_copy(2, i, far_x, ahead_x).wait_recv()
        sb_copy(3, i, far_x, c).start()

    loop(0, chunks, wide_end)

    def sib_end(i):
        sa_copy(0, i, y, 1 - c).wait()
        sb_copy(0, i, x, 1 - c).wait()
        sa_copy(1, i, ahead_y, 1 - c).wait()
        sb_copy(1, i, ahead_x, 1 - c).wait()
        sa_copy(2, i, behind_y, 1 - c).wait()
        sb_copy(2, i, behind_x, 1 - c).wait()
        sa_copy(3, i, far_y, 1 - c).wait()
        sb_copy(3, i, far_x, 1 - c).wait()

    loop(0, chunks, sib_end)

    acch[...] = jnp.zeros_like(acch)
    accq[...] = jnp.zeros_like(accq)

    def project(i):
        zs = pl.ds(4 * lax.rem(i, 4), 4)
        cols = pl.ds(pl.multiple_of(i * STEP, 128), STEP)

        def side(n):
            return gat[n, i // 4, zs].reshape(STEP, 128)

        acch[...] += dot_nn(w13t[:, cols], jnp.concatenate([side(0), side(1)], axis=1))
        accq[...] += dot_nn(w2[:, cols], jnp.concatenate([side(2), side(3)], axis=1))

    loop(0, 16, project)

    low_sums = sum_done(0)
    u1 = low_sums[0:16].astype(BF16)
    u3 = low_sums[16:32].astype(BF16)
    v = low_sums[32:48]
    h1 = acch[0:HID] + SCALE * dot_tn(b1[0], u1)
    h3 = acch[HID : 2 * HID] + SCALE * dot_tn(b3[0], u3)
    q = accq[...] + SCALE * dot_tn(d1t[0], v.astype(BF16))
    sig = jax.nn.sigmoid(h1)
    active = h1 * sig
    slope = sig * (1.0 + h1 * (1.0 - sig))
    hidden = (active * h3).astype(BF16)
    back = weight * q
    e1 = (back * h3 * slope).astype(BF16)
    e3 = (back * active).astype(BF16)
    kk = jnp.sum(hidden.astype(F32) * q, axis=0, keepdims=True)
    et[0:HID, :] = e1
    et[HID : 2 * HID, :] = e3
    sum_start(
        1,
        jnp.concatenate(
            [
                dot_nn(b1[0], e1),
                dot_nn(b3[0], e3),
                dot_nn(d1t[0], hidden),
                kk,
                jnp.zeros((15, NT), F32),
            ],
            axis=0,
        ),
    )

    def grads(i, zoff):
        yy = i // 2
        zz = zoff + 4 * lax.rem(i, 2)
        rows = pl.ds(pl.multiple_of((yy * NZ + zz) * FD, FD), STEP)
        wide = jnp.concatenate([w1[rows, :], w3[rows, :]], axis=1)
        out = dot_nn(wide, et[...]).astype(BF16).reshape(4, 2, HR, NT)
        for rh in range(2):
            for th in range(2):
                yb[2 * rh + th, yy, pl.ds(zz, 4)] = out[:, rh, :, 128 * th : 128 * th + 128]

    mine = 8 * c
    other = 8 - mine
    loop(0, 8, lambda i: grads(i, other))

    def k_copy():
        return remote(yb.at[:, :, pl.ds(other, 8)], rc, k_ss.at[0], k_rs.at[0], sib)

    k_copy().start()
    loop(0, 8, lambda i: grads(i, mine))

    dft[0] = SCALE * dot_nt((weight * v).astype(BF16), hidden)
    gs[0] = SCALE * dot_nt(u1, e1)
    us[0] = SCALE * dot_nt(u3, e3)

    k_copy().wait()

    def add_core(i):
        xx = i // 4
        yy = lax.rem(i, 4)
        both = yb[xx, yy, pl.ds(mine, 8)].astype(F32) + rc[xx, yy].astype(F32)
        yb[xx, yy, pl.ds(mine, 8)] = both.astype(BF16)

    loop(0, 16, add_core)

    def px_copy(i):
        to = lax.rem(x + i, NX)
        return remote(
            yb.at[to, :, pl.ds(mine, 4)], axb.at[i], p1_ss.at[0, i], p1_rs.at[0, i], at_x(to)
        )

    def py_copy(i):
        to = lax.rem(y + i, NY)
        return remote(
            yb.at[:, to, pl.ds(mine + 4, 4)], byb.at[i], p1_ss.at[1, i], p1_rs.at[1, i], at_y(to)
        )

    for i in (1, 3, 2):
        px_copy(i).start()
        py_copy(i).start()

    sum_middle(1)

    for i in (1, 3, 2):
        px_copy(i).wait()
        py_copy(i).wait()

    def add_first(i):
        sa = yb[x, i, pl.ds(mine, 4)].astype(F32)
        sb = yb[i, y, pl.ds(mine + 4, 4)].astype(F32)
        for k in (1, 2, 3):
            sa = sa + axb[k, i].astype(F32)
            sb = sb + byb[k, i].astype(F32)
        ya[i] = sa.astype(BF16)
        yc[i] = sb.astype(BF16)

    loop(0, 4, add_first)

    def qy_copy(i):
        to = lax.rem(y + i, NY)
        return remote(ya.at[to], ayb.at[i], p2_ss.at[0, i], p2_rs.at[0, i], at_y(to))

    def qx_copy(i):
        to = lax.rem(x + i, NX)
        return remote(yc.at[to], bxb.at[i], p2_ss.at[1, i], p2_rs.at[1, i], at_x(to))

    for i in (1, 3, 2):
        qy_copy(i).start()
        qx_copy(i).start()

    sum_last(1)

    for i in (1, 3, 2):
        qy_copy(i).wait()
        qx_copy(i).wait()

    sa = ya[y].astype(F32)
    sb = yc[x].astype(F32)
    for k in (1, 2, 3):
        sa = sa + ayb[k].astype(F32)
        sb = sb + bxb[k].astype(F32)
    zsend[0:4] = sa.astype(BF16)
    zsend[4:8] = sb.astype(BF16)

    holder = z // 8 == c

    def t_copy(k, i, slot):
        return remote(
            zsend.at[k], zr.at[slot], p3_ss.at[k], p3_rs.at[i], at_z(mine + k)
        )

    def t_start(k):
        to = mine + k

        @pl.when(to != z)
        def _():
            t_copy(k, lax.rem(to + NZ - z, NZ), z).start()

    loop(0, 8, t_start)

    sums = sum_done(1)
    r13 = sums[0:32].astype(BF16)
    zt = (weight * sums[32:48]).astype(BF16)
    first = SCALE * dot_nt(r13, xj[...])
    gft[0] = first[0:16]
    uft[0] = first[16:32]
    ds[0] = SCALE * dot_nt(zt, gj[...])
    ascr[FD:128, :] = jnp.zeros((128 - FD, NT), F32)
    ascr[0:FD, :] = SCALE * dot_tn(a13t, r13)
    ascr[FD : FD + 1, :] = sums[48:49]
    asend[...] = jnp.transpose(ascr[...]).astype(BF16).reshape(8, TB, 128)
    afin[e] = asend[e]

    def h_copy(i, slot):
        to = lax.rem(e + i, 8)
        return remote(asend.at[to], afin.at[slot], h_ss.at[i], h_rs.at[i], (to, j))

    loop(1, 8, lambda i: h_copy(i, e).start())

    def t_sent(k):
        @pl.when(mine + k != z)
        def _():
            t_copy(k, 0, z).wait_send()

    loop(0, 8, t_sent)

    rh = x // 2
    th = lax.rem(x, 2)

    def f_copy(i):
        return remote(fsend.at[i], fin.at[rh], f_ss.at[i], f_rs.at[rh], (4 * th + i, j))

    @pl.when(holder)
    def _():
        zr[z] = zsend[lax.rem(z, 8)]

        def got(i):
            t_copy(0, i, lax.rem(z + NZ - i, NZ)).wait_recv()

        loop(1, NZ, got)
        fscr[...] = jnp.zeros_like(fscr)
        fscr[pl.ds(pl.multiple_of(HR * rh, HR), HR), :] = jnp.sum(zr[...].astype(F32), axis=0)
        fsend[...] = jnp.transpose(fscr[...]).astype(BF16).reshape(4, TB, 128)
        for i in range(4):

            @pl.when(4 * th + i == e)
            def _():
                fin[rh] = fsend[i]

            @pl.when(4 * th + i != e)
            def _():
                f_copy(i).start()

    loop(1, 8, lambda i: h_copy(i, lax.rem(e + 8 - i, 8)).wait())

    total = jnp.zeros((TB, 128), F32)
    first_k = jnp.zeros((TB, 1), F32)
    second_k = jnp.zeros((TB, 1), F32)
    for n in range(8):
        block = afin[n].astype(F32)
        total = total + block
        column = block[:, FD : FD + 1]
        first_k = first_k + jnp.where(idv[:, 0:1] == n, column, 0.0)
        second_k = second_k + jnp.where(idv[:, 1:2] == n, column, 0.0)
    cg[:, 0:1] = first_k
    cg[:, 1:2] = second_k

    for n in range(2):

        @pl.when(4 * n + 2 * (e // 4) + z // 8 != e)
        def _():
            remote(fsend.at[0], fin.at[n], f_ss.at[0], f_rs.at[n], (e, j)).wait_recv()

    total = total + fin[0].astype(F32) + fin[1].astype(F32)
    tg[...] = total[:, 0:FD].astype(BF16)

    @pl.when(holder)
    def _():
        for i in range(4):

            @pl.when(4 * th + i != e)
            def _():
                f_copy(i).wait_send()

    for k in range(3):
        a1_copy(k, x, ahead_x).wait_send()
        b1_copy(k, y, ahead_y).wait_send()

        def sent(i):
            a2_copy(k, i, y, ahead_y).wait_send()
            b2_copy(k, i, x, ahead_x).wait_send()

        loop(0, chunks, sent)


def local(
    tokens,
    upstream,
    expert_ids,
    slot_pos,
    combine,
    gate_weight,
    upward_weight,
    down_weight,
    gate_adapter_first,
    gate_adapter_second,
    upward_adapter_first,
    upward_adapter_second,
    down_adapter_first,
    down_right,
):
    vmem = pl.BlockSpec(memory_space=pltpu.VMEM)
    hbm = pl.BlockSpec(memory_space=pl.ANY)
    dma = pltpu.SemaphoreType.DMA

    def buf(shape, dtype=BF16):
        return pltpu.VMEM(shape, dtype)

    chunks = 8 // PAIR
    outs = pl.pallas_call(
        kernel,
        out_shape=(
            jax.ShapeDtypeStruct((TB, FD), BF16),
            jax.ShapeDtypeStruct((TB, 2), F32),
            jax.ShapeDtypeStruct((1, 16, FD), F32),
            jax.ShapeDtypeStruct((1, 16, HID), F32),
            jax.ShapeDtypeStruct((1, 16, FD), F32),
            jax.ShapeDtypeStruct((1, 16, HID), F32),
            jax.ShapeDtypeStruct((1, 16, HID), F32),
            jax.ShapeDtypeStruct((1, 16, FD), F32),
        ),
        in_specs=[vmem] * 4 + [hbm] * 3 + [vmem] * 6,
        out_specs=[vmem] * 8,
        scratch_shapes=[
            buf((6144, HID)),
            buf((6144, HID)),
            buf((HID, 6144)),
            buf((2 * HID, 6144)),
            buf((2 * TB, 128)),
            buf((8, 2 * TB, 128)),
            buf((FD, NT)),
            buf((FD, NT)),
            buf((NX, NC, HR, 128)),
            buf((NX, NY, NZ, NC, HR, 128)),
            buf((2 * HID, NT), F32),
            buf((HID, NT), F32),
            buf((2 * HID, NT)),
            buf((2, NZ, 8, 128), F32),
            buf((2, NZ, 8, 128), F32),
            buf((2, 8, 128), F32),
            buf((2, NY, 8, 128), F32),
            buf((2, NZ, 8, 128), F32),
            buf((NX, NY, NZ, HR, 128)),
            buf((NX, NY, 8, HR, 128)),
            buf((4, NY, 4, HR, 128)),
            buf((4, NX, 4, HR, 128)),
            buf((NY, 4, HR, 128)),
            buf((NX, 4, HR, 128)),
            buf((4, 4, HR, 128)),
            buf((4, 4, HR, 128)),
            buf((8, HR, 128)),
            buf((NZ, HR, 128)),
            buf((128, 128), F32),
            buf((4, TB, 128)),
            buf((2, TB, 128)),
            buf((128, NT), F32),
            buf((8, TB, 128)),
            buf((8, TB, 128)),
            dma((3,)),
            dma((8,)),
            dma((8,)),
            dma((NZ,)),
            dma((NZ,)),
            dma((3,)),
            dma((3,)),
            dma((3,)),
            dma((3,)),
            dma((3, chunks)),
            dma((3, chunks)),
            dma((3, chunks)),
            dma((3, chunks)),
            dma((4, chunks)),
            dma((4, chunks)),
            dma((4, chunks)),
            dma((4, chunks)),
            dma((2, NZ)),
            dma((2, NZ)),
            dma((2, NY)),
            dma((2, NY)),
            dma((2, NZ)),
            dma((2, NZ)),
            dma((1,)),
            dma((1,)),
            dma((2, 4)),
            dma((2, 4)),
            dma((2, 4)),
            dma((2, 4)),
            dma((8,)),
            dma((NZ,)),
            dma((4,)),
            dma((2,)),
            dma((8,)),
            dma((8,)),
        ],
        compiler_params=pltpu.CompilerParams(
            collective_id=0, has_side_effects=True, vmem_limit_bytes=48 * 2**20
        ),
        name="moe_backward",
    )(
        tokens,
        upstream,
        expert_ids,
        combine,
        gate_weight,
        upward_weight,
        down_weight,
        jnp.swapaxes(gate_adapter_first, 1, 2),
        gate_adapter_second,
        jnp.swapaxes(upward_adapter_first, 1, 2),
        upward_adapter_second,
        jnp.swapaxes(down_adapter_first, 1, 2),
        down_right,
    )
    token_grads, combine_grads, gft, gs, uft, us, dft, ds = outs
    return (
        token_grads,
        combine_grads,
        jnp.swapaxes(gft, 1, 2),
        gs,
        jnp.swapaxes(uft, 1, 2),
        us,
        jnp.swapaxes(dft, 1, 2),
        ds,
    )


def solution(mesh):
    in_specs = (
        P("expert", "tensor"),
        P("expert", "tensor"),
        P("expert", None),
        P("expert", None),
        P("expert", None),
        P("expert", None, "tensor"),
        P("expert", None, "tensor"),
        P("expert", "tensor", None),
        P("expert", "tensor", None),
        P("expert", None, "tensor"),
        P("expert", "tensor", None),
        P("expert", None, "tensor"),
        P("expert", "tensor", None),
        P("expert", None, "tensor"),
    )
    out_specs = (
        P("expert", "tensor"),
        P("expert", None),
        P("expert", "tensor", None),
        P("expert", None, "tensor"),
        P("expert", "tensor", None),
        P("expert", None, "tensor"),
        P("expert", "tensor", None),
        P("expert", None, "tensor"),
    )
    return jax.shard_map(local, mesh=mesh, in_specs=in_specs, out_specs=out_specs, check_vma=False)
```

time: 1240 us -> 120 us (0.10)
  blocking collectives: 593 us -> 0 us
  waiting for transfers between devices: 501 us -> 0 us
  Pallas kernels: 0 us -> 103 us
  starting transfers between devices: 67.3 us -> 0 us
  matrix products: 24.8 us -> 0 us
  local copies, waits for them, and re-layouts: 38.6 us -> 16.1 us
  between operations: 14 us -> 0.66 us
    psum x3 -> x0, blocking collectives: 564 us -> none  [the longest x2 336 us: local(): lax.psum((hidden_low, gate_backward, upward_backward, partial_combine), '...]
    unnamed x4 -> x0, waiting for transfers between devices: 460 us -> none
    pallas_call x0 -> x1, Pallas kernels: none -> 103 us  [local(): pl.pallas_call(kernel, out_shape=(jax.ShapeDtypeStruct((TB, FD), BF16), j...]
    all_to_all x2 -> x0, starting transfers between devices: 67.2 us -> none  [the longest x1 51.7 us: local(): lax.all_to_all(grads_comb.astype(jnp.bfloat16), 'expert', split_axis=2, c...]
    all_gather x2 -> x0, waiting for transfers between devices: 33.2 us -> none  [the longest x1 33.1 us: local(): dy_piece = lax.all_gather(local_dy, 'tensor', axis=2, tiled=True)]
    all_to_all x3 -> x0, blocking collectives: 29.5 us -> none  [the longest x1 14 us: local(): lax.all_to_all(to_slots(tokens), 'expert', split_axis=0, concat_axis=1, t...]
    all_gather x2 -> x0, local copies, waits for them, and re-layouts: 26.6 us -> none  [the longest x1 13.3 us: local(): x_piece = lax.all_gather(local_x, 'tensor', axis=2, tiled=True)]
    dot_general x25 -> x0, matrix products: 24.8 us -> none  [the longest x1 3.37 us: local(): jnp.einsum('esc,efc->esf', dy_piece, down_weight, preferred_element_type=...]
  transfers between devices with their start and end apart: 5 -> 0, of which waited for: 4 -> 0; matrix products, arithmetic and copies ran while one was open for 2% -> 0% of each run, Pallas kernels for 0% -> 0%
where the time goes in v1:
time: 120 us
  Pallas kernels  103 us (86%)
  local copies, waits for them, and re-layouts  16.1 us (13%)
    pallas_call x1, Pallas kernels, local(): pl.pallas_call(kernel, out_shape=(jax.ShapeDtypeStruct((TB, FD), BF16), j...  103 us
    unnamed x32, local copies, waits for them, and re-layouts  16.1 us

profile of v1, /device:TPU:1, one launch (start us, length us, event | category | flops | bytes accessed | tf_op | source)
XLA Modules:
  0.0 119.8 jit_solution(15952402590099414862)
XLA Ops:
  0.6 0.8 copy.21.ids
  1.4 0.8 copy.22.comb
  2.2 0.0 copy-start
  2.2 1.4 %copy-done = bf16[1,6144,128]{2,1,0:T(8,128)(2,1)S(1)} copy-done((bf16[1,6144,128]{2,1,0:T(8,128)(2,1)S(1)}, bf16[1,6144,128]{2,1,0:T(8,128)(2,1)}, u32[]{:S(2)}) %copy-start) | copy-done | bytes 1572888
  3.6 0.0 copy-start.1
  3.6 1.4 %copy-done.1 = bf16[1,6144,128]{2,1,0:T(8,128)(2,1)S(1)} copy-done((bf16[1,6144,128]{2,1,0:T(8,128)(2,1)S(1)}, bf16[1,6144,128]{2,1,0:T(8,128)(2,1)}, u32[]{:S(2)}) %copy-start.1) | copy-done | bytes 1572888
  5.0 1.4 %copy-done.2 = bf16[1,128,6144]{2,1,0:T(8,128)(2,1)S(1)} copy-done((bf16[1,128,6144]{2,1,0:T(8,128)(2,1)S(1)}, bf16[1,128,6144]{2,1,0:T(8,128)(2,1)}, u32[]{:S(2)}) %copy-start.2) | copy-done | bytes 1572888
  6.4 0.7 copy-done.3
  7.1 0.7 copy-done.4
  7.8 0.7 copy-done.5
  8.5 0.7 copy-done.6
  9.1 0.7 copy-done.7
  9.8 0.7 copy-done.8
  10.5 0.7 copy-done.9
  11.2 0.7 copy-done.10
  11.9 103.1 %moe_backward.1 = (bf16[32,96]{1,0:T(8,128)(2,1)S(1)}, f32[32,2]{1,0:T(8,128)S(1)}, f32[1,16,96]{2,1,0:T(8,128)S(1)}, f32[1,16,128]{2,1,0:T(8,128)S(1)}, f32[1,1...) custom-call(bf16[32,96]{1,0:T(8,128)(2,1)S(1)} %copy-done.3, ...), custom_call_target="tpu_custom_call" | custom-call | tf_op jit(solution)/shard_map/moe_backward/pallas_call | solution.py:660
  115.0 0.6 copy.23
  115.6 0.6 copy.31
  116.2 0.6 copy.32
  116.8 0.6 copy.33
  117.4 0.6 copy.34
  118.0 0.6 copy.35
  118.6 0.6 copy.36
  119.2 0.6 copy.37
  (9 shorter events, 0.0 us)
Async XLA Ops:
  2.2 1.4 %copy-start = (bf16[1,6144,128]{2,1,0:T(8,128)(2,1)S(1)}, bf16[1,6144,128]{2,1,0:T(8,128)(2,1)}, u32[]{:S(2)}) copy-start(bf16[1,6144,128]{2,1,0:T(8,128)(2,1)} %w1_hbm.1) | copy-start | bytes 4718596
  3.6 1.4 %copy-start.1 = (bf16[1,6144,128]{2,1,0:T(8,128)(2,1)S(1)}, bf16[1,6144,128]{2,1,0:T(8,128)(2,1)}, u32[]{:S(2)}) copy-start(bf16[1,6144,128]{2,1,0:T(8,128)(2,1)} %w3_hbm.1) | copy-start | bytes 4718596
  5.0 1.4 %copy-start.2 = (bf16[1,128,6144]{2,1,0:T(8,128)(2,1)S(1)}, bf16[1,128,6144]{2,1,0:T(8,128)(2,1)}, u32[]{:S(2)}) copy-start(bf16[1,128,6144]{2,1,0:T(8,128)(2,1)} %w2_hbm.1) | copy-start | bytes 4718596
  6.4 0.7 copy-start.3
  7.1 0.7 copy-start.4
  7.8 0.7 copy-start.5
  8.5 0.7 copy-start.6
  9.1 0.7 copy-start.7
  9.8 0.7 copy-start.8
  10.5 0.7 copy-start.9
  11.2 0.7 copy-start.10

commit v2 on v1

v2 whole, which is shorter than its diff:
```python
import jax
import jax.numpy as jnp
from jax import lax
from jax.experimental import pallas as pl
from jax.experimental.pallas import tpu as pltpu
from jax.sharding import PartitionSpec as P

MESH = pl.DeviceIdType.MESH
F32 = jnp.float32
BF16 = jnp.bfloat16
SCALE = 2.0
NX, NY, NZ, NC = 4, 4, 16, 2
TB = 32
FD = 96
HR = 48
HID = 128
NT = 256
STEP = 4 * FD
GRANT = 60 * 2**20
NEAR = 4


def dot_nn(a, b):
    return lax.dot_general(a, b, (((1,), (0,)), ((), ())), preferred_element_type=F32)


def dot_nt(a, b):
    return lax.dot_general(a, b, (((1,), (1,)), ((), ())), preferred_element_type=F32)


def dot_tn(a, b):
    return lax.dot_general(a, b, (((0,), (0,)), ((), ())), preferred_element_type=F32)


def remote(src, dst, send, recv, dev):
    return pltpu.make_async_remote_copy(
        src_ref=src, dst_ref=dst, send_sem=send, recv_sem=recv, device_id=dev, device_id_type=MESH
    )


def loop(low, high, body):
    def step(i, carry):
        body(i)
        return carry

    lax.fori_loop(low, high, step, 0)


def kernel(
    tok_hbm,
    ups_hbm,
    ids_hbm,
    comb_hbm,
    w1_hbm,
    w3_hbm,
    w2_hbm,
    a1t_hbm,
    b1_hbm,
    a3t_hbm,
    b3_hbm,
    d1t_hbm,
    rj_hbm,
    tg,
    cg,
    gft,
    gs,
    uft,
    us,
    dft,
    ds,
    tok,
    ups,
    ids,
    comb,
    a1t,
    b1,
    a3t,
    b3,
    d1t,
    rj,
    w1,
    w3,
    w2,
    w13t,
    wide_t,
    src,
    disp,
    xj,
    gj,
    own,
    gat,
    acch,
    accq,
    et,
    part,
    rsb,
    ysend,
    yrec,
    full,
    yb,
    rc,
    axo,
    byo,
    axr,
    byr,
    ya,
    yc,
    ayb,
    bxb,
    zsend,
    zr,
    fscr,
    fsend,
    fin,
    ascr,
    asend,
    afin,
    w_sem,
    d_ss,
    d_rs,
    z_ss,
    z_rs,
    a1_ss,
    a1_rs,
    b1_ss,
    b1_rs,
    a2_ss,
    a2_rs,
    b2_ss,
    b2_rs,
    s1_ss,
    s1_rs,
    s2_ss,
    s2_rs,
    r_ss,
    r_rs,
    y_ss,
    y_rs,
    g_ss,
    g_rs,
    k_ss,
    k_rs,
    p1_ss,
    p1_rs,
    p2_ss,
    p2_rs,
    p3_ss,
    p3_rs,
    f_ss,
    f_rs,
    h_ss,
    h_rs,
    known,
):
    e = lax.axis_index("expert")
    j = lax.axis_index("tensor")
    x = e // 2
    c = lax.rem(e, 2)
    y = j // NZ
    z = lax.rem(j, NZ)
    sib = (2 * x + 1 - c, j)

    def at_x(v):
        return (2 * v + c, j)

    def at_y(v):
        return (e, v * NZ + z)

    def at_z(v):
        return (e, y * NZ + v)

    bar = pltpu.get_barrier_semaphore()

    def sig_e(i):
        pl.semaphore_signal(bar, inc=1, device_id=(lax.rem(e + i, 8), j), device_id_type=MESH)

    def sig_z(i):
        pl.semaphore_signal(bar, inc=1, device_id=at_z(lax.rem(z + i, NZ)), device_id_type=MESH)

    def sig_y(i):
        pl.semaphore_signal(bar, inc=1, device_id=at_y(lax.rem(y + i, NY)), device_id_type=MESH)

    loop(1, NEAR + 1, sig_z)
    loop(NZ - NEAR, NZ, sig_z)
    loop(1, NY, sig_y)
    loop(1, 8, sig_e)

    pairs = [
        (tok_hbm, tok),
        (ups_hbm, ups),
        (ids_hbm, ids),
        (comb_hbm, comb),
        (a1t_hbm, a1t),
        (b1_hbm, b1),
        (a3t_hbm, a3t),
        (b3_hbm, b3),
        (d1t_hbm, d1t),
        (rj_hbm, rj),
        (w1_hbm.at[0], w1),
        (w3_hbm.at[0], w3),
        (w2_hbm.at[0], w2),
    ]
    loads = [pltpu.make_async_copy(a, b, w_sem.at[n]) for n, (a, b) in enumerate(pairs)]
    for load in loads:
        load.start()
    for load in loads[0:4]:
        load.wait()

    expert_row = lax.broadcasted_iota(jnp.int32, (8, TB), 0)
    dense = jnp.zeros((8, TB), F32)
    for k in range(2):
        dense = dense + jnp.where(expert_row == ids[k : k + 1, :], comb[k : k + 1, :], 0.0)
    high = dense.astype(BF16).astype(F32)
    wide_t[...] = jnp.zeros_like(wide_t)
    wide_t[0:2, 0:TB] = ids[...].astype(F32)
    wide_t[FD : FD + 8, 0:TB] = high
    wide_t[FD + 8 : FD + 16, 0:TB] = dense - high
    wide = jnp.transpose(wide_t[...])[0:TB, :]
    id0 = wide[:, 0:1]
    id1 = wide[:, 1:2]
    src[0:TB, :] = wide.astype(BF16)
    src[0:TB, 0:FD] = tok[...]
    src[TB : 2 * TB, :] = jnp.zeros((TB, 128), BF16)
    src[TB : 2 * TB, 0:FD] = ups[...]
    disp[e] = src[...]
    for load in loads[4:]:
        load.wait()

    def flip(i):
        rows = pl.ds(pl.multiple_of(i * 128, 128), 128)
        w13t[0:HID, rows] = jnp.transpose(w1[rows, :])
        w13t[HID : 2 * HID, rows] = jnp.transpose(w3[rows, :])


    pl.semaphore_wait(bar, 7 + 2 * NEAR + NY - 1)

    def disp_copy(i, slot):
        return remote(
            src, disp.at[slot], d_ss.at[i], d_rs.at[i], (lax.rem(e + i, 8), j)
        )

    loop(1, 8, lambda i: disp_copy(i, e).start())
    for step in (NEAR, NZ - NEAR):
        pl.semaphore_signal(
            known, inc=1, device_id=at_z(lax.rem(z + step, NZ)), device_id_type=MESH
        )
    loop(1, 8, lambda i: disp_copy(i, lax.rem(e + 8 - i, 8)).wait())

    xt = jnp.transpose(disp[:, 0:TB, :].reshape(NT, 128))
    gt = jnp.transpose(disp[:, TB : 2 * TB, :].reshape(NT, 128))
    row = lax.broadcasted_iota(jnp.int32, (32, NT), 0)
    tail = xt[FD:128, :].astype(F32)
    weight = jnp.sum(jnp.where((row == e) | (row == e + 8), tail, 0.0), axis=0, keepdims=True)
    xj[...] = xt[0:FD, :]
    gj[...] = gt[0:FD, :]
    for half in range(2):
        for th in range(2):
            cut = slice(128 * th, 128 * th + 128)
            rows = slice(HR * half, HR * half + HR)
            own[th, half] = xt[rows, cut]
            own[2 + th, half] = gt[rows, cut]
    gat[x, y, z, c] = own[x, c]

    pl.semaphore_wait(known, 2)

    def z_copy(of, to):
        piece = gat.at[x, y, of, c]
        return remote(piece, piece, z_ss.at[to], z_rs.at[of], at_z(to))

    group = z // 4
    for off in (0, 3, 1, 2):

        def z_start(i):
            to = 4 * lax.rem(group + off, 4) + i

            @pl.when(to != z)
            def _():
                z_copy(z, to).start()

        loop(0, 4, z_start)

    def sum_start(n, value):
        for k in range(NZ):
            part[n, k] = value[8 * (k // 2) : 8 * (k // 2) + 8, 128 * (k % 2) : 128 * (k % 2) + 128]
        rsb[n, z] = part[n, z]

        def go(i):
            to = lax.rem(z + i, NZ)
            remote(part.at[n, to], rsb.at[n, z], r_ss.at[n, i], r_rs.at[n, i], at_z(to)).start()

        loop(1, NZ, go)

    def y_copy(n, i, slot):
        return remote(
            ysend.at[n], yrec.at[n, slot], y_ss.at[n, i], y_rs.at[n, i], at_y(lax.rem(y + i, NY))
        )

    def sum_middle(n):
        def done(i):
            to = lax.rem(z + i, NZ)
            remote(
                part.at[n, to],
                rsb.at[n, lax.rem(z + NZ - i, NZ)],
                r_ss.at[n, i],
                r_rs.at[n, i],
                at_z(to),
            ).wait()

        loop(1, NZ, done)
        total = jnp.sum(rsb[n], axis=0)
        ysend[n] = total
        yrec[n, y] = total
        loop(1, NY, lambda i: y_copy(n, i, y).start())

    def g_copy(n, i, slot):
        piece = full.at[n, slot]
        return remote(piece, piece, g_ss.at[n, i], g_rs.at[n, i], at_z(lax.rem(z + i, NZ)))

    def sum_last(n):
        loop(1, NY, lambda i: y_copy(n, i, lax.rem(y + NY - i, NY)).wait())
        full[n, z] = jnp.sum(yrec[n], axis=0)
        loop(1, NZ, lambda i: g_copy(n, i, z).start())

    def sum_done(n):
        loop(1, NZ, lambda i: g_copy(n, i, lax.rem(z + NZ - i, NZ)).wait())
        return jnp.concatenate(
            [jnp.concatenate([full[n, 2 * k], full[n, 2 * k + 1]], axis=1) for k in range(8)], axis=0
        )

    a13t = jnp.concatenate([a1t[0], a3t[0]], axis=0)
    sum_start(
        0,
        jnp.concatenate(
            [dot_nn(a13t, xj[...]), dot_nn(rj[0], gj[...]), jnp.zeros((16, NT), F32)], axis=0
        ),
    )

    ahead_x = lax.rem(x + 1 + 2 * c, NX)
    behind_x = lax.rem(x + 3 + 2 * c, NX)
    far_x = lax.rem(x + 2, NX)
    ahead_y = lax.rem(y + 1 + 2 * c, NY)
    behind_y = lax.rem(y + 3 + 2 * c, NY)
    far_y = lax.rem(y + 2, NY)

    def group_of(s):
        n = s // 2
        return lax.rem(group + n + n // 2 - 2 * (n // 3), 4)

    def z_of(s, k):
        return 4 * group_of(s) + 2 * lax.rem(s, 2) + k

    def a1_copy(k, s, of, to):
        piece = gat.at[of, y, z_of(s, 0), c]
        return remote(piece, piece, a1_ss.at[k, s], a1_rs.at[k, s], at_x(to))

    def b1_copy(k, s, of, to):
        piece = gat.at[x, of, z_of(s, 1), c]
        return remote(piece, piece, b1_ss.at[k, s], b1_rs.at[k, s], at_y(to))

    def a2_copy(k, s, of, to):
        piece = gat.at[:, of, z_of(s, 0), c]
        return remote(piece, piece, a2_ss.at[k, s], a2_rs.at[k, s], at_y(to))

    def b2_copy(k, s, of, to):
        piece = gat.at[of, :, z_of(s, 1), c]
        return remote(piece, piece, b2_ss.at[k, s], b2_rs.at[k, s], at_x(to))

    def sa_copy(k, s, of, core):
        piece = gat.at[:, of, z_of(s, 0), core]
        return remote(piece, piece, s1_ss.at[k, s], s1_rs.at[k, s], sib)

    def sb_copy(k, s, of, core):
        piece = gat.at[of, :, z_of(s, 1), core]
        return remote(piece, piece, s2_ss.at[k, s], s2_rs.at[k, s], sib)

    def narrow_start(s):
        for k in range(2):
            of = z_of(s, k)

            @pl.when(of != z)
            def _():
                z_copy(of, z).wait_recv()

        a1_copy(0, s, x, ahead_x).start()
        b1_copy(0, s, y, ahead_y).start()
        a1_copy(1, s, x, behind_x).start()
        b1_copy(1, s, y, behind_y).start()

    def narrow_pass(s):
        a1_copy(0, s, behind_x, ahead_x).wait_recv()
        a1_copy(2, s, behind_x, ahead_x).start()
        b1_copy(0, s, behind_y, ahead_y).wait_recv()
        b1_copy(2, s, behind_y, ahead_y).start()

    def wide_start(s):
        a1_copy(1, s, ahead_x, behind_x).wait_recv()
        a1_copy(2, s, far_x, ahead_x).wait_recv()
        a2_copy(0, s, y, ahead_y).start()
        a2_copy(1, s, y, behind_y).start()
        b1_copy(1, s, ahead_y, behind_y).wait_recv()
        b1_copy(2, s, far_y, ahead_y).wait_recv()
        b2_copy(0, s, x, ahead_x).start()
        b2_copy(1, s, x, behind_x).start()
        sa_copy(0, s, y, c).start()
        sb_copy(0, s, x, c).start()

    def wide_pass(s):
        a2_copy(0, s, behind_y, ahead_y).wait_recv()
        a2_copy(2, s, behind_y, ahead_y).start()
        b2_copy(0, s, behind_x, ahead_x).wait_recv()
        b2_copy(2, s, behind_x, ahead_x).start()
        sa_copy(1, s, behind_y, c).start()
        sb_copy(1, s, behind_x, c).start()
        a2_copy(1, s, ahead_y, behind_y).wait_recv()
        sa_copy(2, s, ahead_y, c).start()
        b2_copy(1, s, ahead_x, behind_x).wait_recv()
        sb_copy(2, s, ahead_x, c).start()

    def wide_end(s):
        a2_copy(2, s, far_y, ahead_y).wait_recv()
        sa_copy(3, s, far_y, c).start()
        b2_copy(2, s, far_x, ahead_x).wait_recv()
        sb_copy(3, s, far_x, c).start()

    def core_end(s):
        for k, (fy, fx) in enumerate(
            ((y, x), (ahead_y, ahead_x), (behind_y, behind_x), (far_y, far_x))
        ):
            sa_copy(k, s, fy, 1 - c).wait()
            sb_copy(k, s, fx, 1 - c).wait()

    def project(s):
        g = group_of(s)

        def one(yy):
            cols = pl.ds(pl.multiple_of((4 * yy + g) * STEP, 128), STEP)

            def side(n):
                return gat[n, yy, pl.ds(4 * g, 4)].reshape(STEP, 128)

            acch[...] += dot_nn(w13t[:, cols], jnp.concatenate([side(0), side(1)], axis=1))
            accq[...] += dot_nn(w2[:, cols], jnp.concatenate([side(2), side(3)], axis=1))

        loop(0, NY, one)

    acch[...] = jnp.zeros_like(acch)
    accq[...] = jnp.zeros_like(accq)

    def at_tick(t, lag, body):
        @pl.when((t >= lag) & (t < lag + 8))
        def _():
            body(t - lag)

    def gather_tick(t):
        at_tick(t, 0, narrow_start)
        at_tick(t, 2, narrow_pass)
        at_tick(t, 4, wide_start)
        at_tick(t, 6, wide_pass)
        at_tick(t, 8, wide_end)
        at_tick(t, 9, core_end)
        at_tick(t, 0, lambda s: loop(6 * s, 6 * s + 6, flip))

        @pl.when((t >= 9) & (lax.rem(t, 2) == 0))
        def _():
            project(t - 9)

        @pl.when(t == 6)
        def _():
            sum_middle(0)

        @pl.when(t == 9)
        def _():
            sum_last(0)

    loop(0, 17, gather_tick)

    low_sums = sum_done(0)
    u1 = low_sums[0:16].astype(BF16)
    u3 = low_sums[16:32].astype(BF16)
    v = low_sums[32:48]
    h1 = acch[0:HID] + SCALE * dot_tn(b1[0], u1)
    h3 = acch[HID : 2 * HID] + SCALE * dot_tn(b3[0], u3)
    q = accq[...] + SCALE * dot_tn(d1t[0], v.astype(BF16))
    sig = jax.nn.sigmoid(h1)
    active = h1 * sig
    slope = sig * (1.0 + h1 * (1.0 - sig))
    hidden = (active * h3).astype(BF16)
    back = weight * q
    e1 = (back * h3 * slope).astype(BF16)
    e3 = (back * active).astype(BF16)
    kk = jnp.sum(hidden.astype(F32) * q, axis=0, keepdims=True)
    et[0:HID, :] = e1
    et[HID : 2 * HID, :] = e3
    sum_start(
        1,
        jnp.concatenate(
            [
                dot_nn(b1[0], e1),
                dot_nn(b3[0], e3),
                dot_nn(d1t[0], hidden),
                kk,
                jnp.zeros((15, NT), F32),
            ],
            axis=0,
        ),
    )

    def group_at(s):
        return lax.rem(group + 2 + s + (s // 2) * (1 - 2 * s), 4)

    def piece_z(s, k, core):
        return 4 * group_at(s) + 2 * core + k

    def k_copy(s, core):
        return remote(
            yb.at[:, :, pl.ds(piece_z(s, 0, core), 2)], rc.at[s], k_ss.at[s], k_rs.at[s], sib
        )

    def grads(s):
        g = group_at(s)

        def one(yy):
            rows = pl.ds(pl.multiple_of((4 * yy + g) * STEP, STEP), STEP)
            pair = jnp.concatenate([w1[rows, :], w3[rows, :]], axis=1)
            out = dot_nn(pair, et[...]).astype(BF16).reshape(4, 2, HR, NT)
            for rh in range(2):
                for th in range(2):
                    yb[2 * rh + th, yy, pl.ds(4 * g, 4)] = out[:, rh, :, 128 * th : 128 * th + 128]

        loop(0, NY, one)
        k_copy(s, 1 - c).start()

    def xo_copy(s):
        return remote(
            yb.at[far_x, :, piece_z(s, 0, c)], axo.at[s], p1_ss.at[0, s], p1_rs.at[0, s], at_x(ahead_x)
        )

    def yo_copy(s):
        return remote(
            yb.at[:, far_y, piece_z(s, 1, c)], byo.at[s], p1_ss.at[1, s], p1_rs.at[1, s], at_y(ahead_y)
        )

    def xr_copy(k, s, to):
        return remote(
            yb.at[to, :, piece_z(s, 0, c)], axr.at[k, s], p1_ss.at[2 + k, s], p1_rs.at[2 + k, s], at_x(to)
        )

    def yr_copy(k, s, to):
        return remote(
            yb.at[:, to, piece_z(s, 1, c)], byr.at[k, s], p1_ss.at[4 + k, s], p1_rs.at[4 + k, s], at_y(to)
        )

    def add_core(s):
        k_copy(s, 1 - c).wait()

        def one(xx):
            zs = pl.ds(piece_z(s, 0, c), 2)
            both = yb[xx, :, zs].astype(F32) + rc[s, xx].astype(F32)
            yb[xx, :, zs] = both.astype(BF16)

        loop(0, NX, one)
        xo_copy(s).start()
        yo_copy(s).start()
        xr_copy(1, s, behind_x).start()
        yr_copy(1, s, behind_y).start()

    def add_far(s):
        za = piece_z(s, 0, c)
        zb = piece_z(s, 1, c)
        xo_copy(s).wait_recv()
        yb[ahead_x, :, za] = (yb[ahead_x, :, za].astype(F32) + axo[s].astype(F32)).astype(BF16)
        xr_copy(0, s, ahead_x).start()
        yo_copy(s).wait_recv()
        yb[:, ahead_y, zb] = (yb[:, ahead_y, zb].astype(F32) + byo[s].astype(F32)).astype(BF16)
        yr_copy(0, s, ahead_y).start()

    def qy_copy(s, i):
        to = lax.rem(y + i, NY)
        return remote(ya.at[s, to], ayb.at[s, i], p2_ss.at[0, s, i], p2_rs.at[0, s, i], at_y(to))

    def qx_copy(s, i):
        to = lax.rem(x + i, NX)
        return remote(yc.at[s, to], bxb.at[s, i], p2_ss.at[1, s, i], p2_rs.at[1, s, i], at_x(to))

    def add_first(s):
        xr_copy(0, s, ahead_x).wait_recv()
        xr_copy(1, s, behind_x).wait_recv()
        ya[s] = (
            yb[x, :, piece_z(s, 0, c)].astype(F32) + axr[0, s].astype(F32) + axr[1, s].astype(F32)
        ).astype(BF16)
        for i in (2, 1, 3):
            qy_copy(s, i).start()
        yr_copy(0, s, ahead_y).wait_recv()
        yr_copy(1, s, behind_y).wait_recv()
        yc[s] = (
            yb[:, y, piece_z(s, 1, c)].astype(F32) + byr[0, s].astype(F32) + byr[1, s].astype(F32)
        ).astype(BF16)
        for i in (2, 1, 3):
            qx_copy(s, i).start()

    def t_copy(s, k):
        to = piece_z(s, k, c)
        return remote(zsend.at[s, k], zr.at[z], p3_ss.at[2 * s + k], p3_rs.at[z], at_z(to))

    def add_second(s):
        for k in range(2):
            for i in (1, 3, 2):
                if k == 0:
                    qy_copy(s, i).wait()
                else:
                    qx_copy(s, i).wait()
            piece = (ya[s, y] if k == 0 else yc[s, x]).astype(F32)
            for i in (1, 2, 3):
                piece = piece + (ayb[s, i] if k == 0 else bxb[s, i]).astype(F32)
            zsend[s, k] = piece.astype(BF16)
            to = piece_z(s, k, c)

            @pl.when(to != z)
            def _():
                t_copy(s, k).start()

            @pl.when(to == z)
            def _():
                zr[z] = zsend[s, k]

    def at_step(t, lag, body):
        @pl.when((t >= lag) & (t < lag + 4))
        def _():
            body(t - lag)

    def scatter_tick(t):
        at_step(t, 0, grads)
        at_step(t, 4, add_second)
        at_step(t, 3, add_first)
        at_step(t, 2, add_far)
        at_step(t, 1, add_core)

        @pl.when(t == 3)
        def _():
            sum_middle(1)

        @pl.when(t == 4)
        def _():
            dft[0] = SCALE * dot_nt((weight * v).astype(BF16), hidden)
            gs[0] = SCALE * dot_nt(u1, e1)
            us[0] = SCALE * dot_nt(u3, e3)

        @pl.when(t == 5)
        def _():
            sum_last(1)

    loop(0, 8, scatter_tick)

    holder = lax.rem(z, 4) // 2 == c
    sums = sum_done(1)
    r13 = sums[0:32].astype(BF16)
    zt = (weight * sums[32:48]).astype(BF16)
    ascr[FD:128, :] = jnp.zeros((128 - FD, NT), F32)
    ascr[0:FD, :] = SCALE * dot_tn(a13t, r13)
    ascr[FD : FD + 1, :] = sums[48:49]
    asend[...] = jnp.transpose(ascr[...]).astype(BF16).reshape(8, TB, 128)
    afin[e] = asend[e]

    def h_copy(i, slot):
        to = lax.rem(e + i, 8)
        return remote(asend.at[to], afin.at[slot], h_ss.at[i], h_rs.at[i], (to, j))

    loop(1, 8, lambda i: h_copy(i, e).start())
    first = SCALE * dot_nt(r13, xj[...])
    gft[0] = first[0:16]
    uft[0] = first[16:32]
    ds[0] = SCALE * dot_nt(zt, gj[...])

    rh = x // 2
    th = lax.rem(x, 2)

    def f_copy(i):
        return remote(fsend.at[i], fin.at[rh], f_ss.at[i], f_rs.at[rh], (4 * th + i, j))

    @pl.when(holder)
    def _():
        def got(i):
            of = lax.rem(z + i, NZ)
            remote(zsend.at[0, 0], zr.at[of], p3_ss.at[0], p3_rs.at[of], at_z(of)).wait_recv()

        loop(1, NZ, got)
        fscr[...] = jnp.zeros_like(fscr)
        fscr[pl.ds(pl.multiple_of(HR * rh, HR), HR), :] = jnp.sum(zr[...].astype(F32), axis=0)
        fsend[...] = jnp.transpose(fscr[...]).astype(BF16).reshape(4, TB, 128)
        for i in range(4):

            @pl.when(4 * th + i == e)
            def _():
                fin[rh] = fsend[i]

            @pl.when(4 * th + i != e)
            def _():
                f_copy(i).start()

    loop(1, 8, lambda i: h_copy(i, lax.rem(e + 8 - i, 8)).wait())

    total = jnp.zeros((TB, 128), F32)
    first_k = jnp.zeros((TB, 1), F32)
    second_k = jnp.zeros((TB, 1), F32)
    for n in range(8):
        block = afin[n].astype(F32)
        total = total + block
        column = block[:, FD : FD + 1]
        first_k = first_k + jnp.where(id0 == n, column, 0.0)
        second_k = second_k + jnp.where(id1 == n, column, 0.0)
    lane = lax.broadcasted_iota(jnp.int32, (TB, 128), 1)
    both_k = jnp.where(lane == 0, first_k, 0.0) + jnp.where(lane == 1, second_k, 0.0)
    cg[...] = jnp.transpose(both_k)[0:2, :]

    for n in range(2):

        @pl.when(4 * n + 2 * (e // 4) + lax.rem(z, 4) // 2 != e)
        def _():
            remote(fsend.at[0], fin.at[n], f_ss.at[0], f_rs.at[n], (e, j)).wait_recv()

    total = total + fin[0].astype(F32) + fin[1].astype(F32)
    tg[...] = total[:, 0:FD].astype(BF16)

    @pl.when(holder)
    def _():
        for i in range(4):

            @pl.when(4 * th + i != e)
            def _():
                f_copy(i).wait_send()

    def z_sent(i):
        z_copy(z, lax.rem(z + i, NZ)).wait_send()

    loop(1, NZ, z_sent)

    def gather_sent(s):
        for k in range(3):
            a1_copy(k, s, x, ahead_x).wait_send()
            b1_copy(k, s, y, ahead_y).wait_send()
            a2_copy(k, s, y, ahead_y).wait_send()
            b2_copy(k, s, x, ahead_x).wait_send()

    loop(0, 8, gather_sent)

    def scatter_sent(s):
        xo_copy(s).wait_send()
        yo_copy(s).wait_send()
        for k in range(2):
            xr_copy(k, s, ahead_x).wait_send()
            yr_copy(k, s, ahead_y).wait_send()

            @pl.when(piece_z(s, k, c) != z)
            def _():
                t_copy(s, k).wait_send()

    loop(0, 4, scatter_sent)


def finish(*refs):
    sems = refs[16]
    copies = [pltpu.make_async_copy(refs[n], refs[8 + n], sems.at[n]) for n in range(8)]
    for copy in copies:
        copy.start()
    for copy in copies:
        copy.wait()


def local(
    tokens,
    upstream,
    expert_ids,
    slot_pos,
    combine,
    gate_weight,
    upward_weight,
    down_weight,
    gate_adapter_first,
    gate_adapter_second,
    upward_adapter_first,
    upward_adapter_second,
    down_adapter_first,
    down_right,
):
    vmem = pl.BlockSpec(memory_space=pltpu.VMEM)
    hbm = pl.BlockSpec(memory_space=pl.ANY)
    dma = pltpu.SemaphoreType.DMA

    def buf(shape, dtype=BF16):
        return pltpu.VMEM(shape, dtype)

    outs = pl.pallas_call(
        kernel,
        out_shape=(
            jax.ShapeDtypeStruct((TB, FD), BF16),
            jax.ShapeDtypeStruct((2, TB), F32),
            jax.ShapeDtypeStruct((1, 16, FD), F32),
            jax.ShapeDtypeStruct((1, 16, HID), F32),
            jax.ShapeDtypeStruct((1, 16, FD), F32),
            jax.ShapeDtypeStruct((1, 16, HID), F32),
            jax.ShapeDtypeStruct((1, 16, HID), F32),
            jax.ShapeDtypeStruct((1, 16, FD), F32),
        ),
        in_specs=[hbm] * 13,
        out_specs=[vmem] * 8,
        scratch_shapes=[
            buf((TB, FD)),
            buf((TB, FD)),
            buf((2, TB), jnp.int32),
            buf((2, TB), F32),
            buf((1, 16, FD)),
            buf((1, 16, HID)),
            buf((1, 16, FD)),
            buf((1, 16, HID)),
            buf((1, 16, HID)),
            buf((1, 16, FD)),
            buf((6144, HID)),
            buf((6144, HID)),
            buf((HID, 6144)),
            buf((2 * HID, 6144)),
            buf((128, 128), F32),
            buf((2 * TB, 128)),
            buf((8, 2 * TB, 128)),
            buf((FD, NT)),
            buf((FD, NT)),
            buf((NX, NC, HR, 128)),
            buf((NX, NY, NZ, NC, HR, 128)),
            buf((2 * HID, NT), F32),
            buf((HID, NT), F32),
            buf((2 * HID, NT)),
            buf((2, NZ, 8, 128), F32),
            buf((2, NZ, 8, 128), F32),
            buf((2, 8, 128), F32),
            buf((2, NY, 8, 128), F32),
            buf((2, NZ, 8, 128), F32),
            buf((NX, NY, NZ, HR, 128)),
            buf((4, NX, NY, 2, HR, 128)),
            buf((4, NY, HR, 128)),
            buf((4, NX, HR, 128)),
            buf((2, 4, NY, HR, 128)),
            buf((2, 4, NX, HR, 128)),
            buf((4, NY, HR, 128)),
            buf((4, NX, HR, 128)),
            buf((4, 4, HR, 128)),
            buf((4, 4, HR, 128)),
            buf((4, 2, HR, 128)),
            buf((NZ, HR, 128)),
            buf((128, 128), F32),
            buf((4, TB, 128)),
            buf((2, TB, 128)),
            buf((128, NT), F32),
            buf((8, TB, 128)),
            buf((8, TB, 128)),
            dma((13,)),
            dma((8,)),
            dma((8,)),
            dma((NZ,)),
            dma((NZ,)),
            dma((3, 8)),
            dma((3, 8)),
            dma((3, 8)),
            dma((3, 8)),
            dma((3, 8)),
            dma((3, 8)),
            dma((3, 8)),
            dma((3, 8)),
            dma((4, 8)),
            dma((4, 8)),
            dma((4, 8)),
            dma((4, 8)),
            dma((2, NZ)),
            dma((2, NZ)),
            dma((2, NY)),
            dma((2, NY)),
            dma((2, NZ)),
            dma((2, NZ)),
            dma((4,)),
            dma((4,)),
            dma((6, 4)),
            dma((6, 4)),
            dma((2, 4, 4)),
            dma((2, 4, 4)),
            dma((8,)),
            dma((NZ,)),
            dma((4,)),
            dma((2,)),
            dma((8,)),
            dma((8,)),
            pltpu.SemaphoreType.REGULAR,
        ],
        compiler_params=pltpu.CompilerParams(
            collective_id=0, has_side_effects=True, vmem_limit_bytes=GRANT
        ),
        name="moe_backward",
    )(
        tokens,
        upstream,
        jnp.transpose(expert_ids),
        jnp.transpose(combine),
        gate_weight,
        upward_weight,
        down_weight,
        jnp.swapaxes(gate_adapter_first, 1, 2),
        gate_adapter_second,
        jnp.swapaxes(upward_adapter_first, 1, 2),
        upward_adapter_second,
        jnp.swapaxes(down_adapter_first, 1, 2),
        down_right,
    )
    token_grads, combine_grads, gft, gs, uft, us, dft, ds = pl.pallas_call(
        finish,
        out_shape=[jax.ShapeDtypeStruct(o.shape, o.dtype) for o in outs],
        in_specs=[hbm] * 8,
        out_specs=[hbm] * 8,
        scratch_shapes=[dma((8,))],
        compiler_params=pltpu.CompilerParams(vmem_limit_bytes=GRANT),
        name="hand_over",
    )(*outs)
    return (
        token_grads,
        jnp.transpose(combine_grads),
        jnp.swapaxes(gft, 1, 2),
        gs,
        jnp.swapaxes(uft, 1, 2),
        us,
        jnp.swapaxes(dft, 1, 2),
        ds,
    )


def solution(mesh):
    in_specs = (
        P("expert", "tensor"),
        P("expert", "tensor"),
        P("expert", None),
        P("expert", None),
        P("expert", None),
        P("expert", None, "tensor"),
        P("expert", None, "tensor"),
        P("expert", "tensor", None),
        P("expert", "tensor", None),
        P("expert", None, "tensor"),
        P("expert", "tensor", None),
        P("expert", None, "tensor"),
        P("expert", "tensor", None),
        P("expert", None, "tensor"),
    )
    out_specs = (
        P("expert", "tensor"),
        P("expert", None),
        P("expert", "tensor", None),
        P("expert", None, "tensor"),
        P("expert", "tensor", None),
        P("expert", None, "tensor"),
        P("expert", "tensor", None),
        P("expert", None, "tensor"),
    )
    return jax.shard_map(local, mesh=mesh, in_specs=in_specs, out_specs=out_specs, check_vma=False)
```

time: 120 us -> 98.9 us (0.82)
  local copies, waits for them, and re-layouts: 16.1 us -> 0 us
  Pallas kernels: 103 us -> 98.1 us
    unnamed x32 -> x0, local copies, waits for them, and re-layouts: 16.1 us -> none
    pallas_call x1, Pallas kernels: 103 us -> 95.2 us  [local(): pl.pallas_call(kernel, out_shape=(jax.ShapeDtypeStruct((TB, FD), BF16), j...]
    pallas_call x0 -> x1, Pallas kernels: none -> 2.95 us  [local(): pl.pallas_call(finish, out_shape=[jax.ShapeDtypeStruct(o.shape, o.dtype)...]
where the time goes in v2:
time: 98.9 us; the launch traced here: 98.7 us
  Pallas kernels  98.1 us (99%)
    pallas_call x1, Pallas kernels, local(): pl.pallas_call(kernel, out_shape=(jax.ShapeDtypeStruct((TB, FD), BF16), j...  95.2 us
    pallas_call x1, Pallas kernels, local(): pl.pallas_call(finish, out_shape=[jax.ShapeDtypeStruct(o.shape, o.dtype)...  2.95 us

profile of v2, /device:TPU:1, one launch (start us, length us, event | category | flops | bytes accessed | tf_op | source)
XLA Modules:
  0.0 98.7 jit_solution(6982338324343298809)
XLA Ops:
  0.6 95.2 %moe_backward.1 = (bf16[32,96]{1,0:T(8,128)(2,1)}, f32[2,32]{1,0:T(2,128)}, f32[1,16,96]{2,1,0:T(8,128)}, f32[1,16,128]{2,1,0:T(8,128)}, f32[1,16,96]{2,1,0:T(8,...) custom-call(bf16[32,96]{1,0:T(8,128)(2,1)} %tok_hbm.1, bf16[32,96]{1,0:T(8,128)(2,1)} %ups_hbm.1, ...), custom_call_target="tpu_custom_call" | custom-call | tf_op jit(solution)/shard_map/moe_backward/pallas_call | solution.py:792
  95.8 2.9 %hand_over.1 = (bf16[32,96]{1,0:T(8,128)(2,1)}, f32[2,32]{1,0:T(2,128)}, f32[1,16,96]{2,1,0:T(8,128)}, f32[1,16,128]{2,1,0:T(8,128)}, f32[1,16,96]{2,1,0:T(8,128...) custom-call(bf16[32,96]{1,0:T(8,128)(2,1)} %get-tuple-element.24.refs_0_, ...), custom_call_target="tpu_custom_call" | custom-call | tf_op jit(solution)/shard_map/hand_over/pallas_call | solution.py:910

commit v3 on v2

--- a/solution.py
+++ b/solution.py
@@ -120,18 +120,12 @@
     d_rs,
     z_ss,
     z_rs,
-    a1_ss,
-    a1_rs,
-    b1_ss,
-    b1_rs,
-    a2_ss,
-    a2_rs,
-    b2_ss,
-    b2_rs,
-    s1_ss,
-    s1_rs,
-    s2_ss,
-    s2_rs,
+    n_ss,
+    n_rs,
+    w_ss,
+    w_rs,
+    c_ss,
+    c_rs,
     r_ss,
     r_rs,
     y_ss,
@@ -169,6 +163,15 @@
     def at_z(v):
         return (e, y * NZ + v)
 
+    def arrived(ref, sem):
+        remote(ref, ref, sem, sem, sib).wait_recv()
+
+    def left(ref, sem):
+        remote(ref, ref, sem, sem, sib).wait_send()
+
+    def pieces(n):
+        return gat.at[0, 0, 0:n, 0]
+
     bar = pltpu.get_barrier_semaphore()
 
     def sig_e(i):
@@ -232,11 +235,12 @@
         w13t[HID : 2 * HID, rows] = jnp.transpose(w3[rows, :])
 
 
+    loop(0, 24, flip)
     pl.semaphore_wait(bar, 7 + 2 * NEAR + NY - 1)
 
     def disp_copy(i, slot):
         return remote(
-            src, disp.at[slot], d_ss.at[i], d_rs.at[i], (lax.rem(e + i, 8), j)
+            src, disp.at[slot], d_ss.at[0], d_rs.at[0], (lax.rem(e + i, 8), j)
         )
 
     loop(1, 8, lambda i: disp_copy(i, e).start())
@@ -244,7 +248,7 @@
         pl.semaphore_signal(
             known, inc=1, device_id=at_z(lax.rem(z + step, NZ)), device_id_type=MESH
         )
-    loop(1, 8, lambda i: disp_copy(i, lax.rem(e + 8 - i, 8)).wait())
+    arrived(disp.at[0:7], d_rs.at[0])
 
     xt = jnp.transpose(disp[:, 0:TB, :].reshape(NT, 128))
     gt = jnp.transpose(disp[:, TB : 2 * TB, :].reshape(NT, 128))
@@ -265,7 +269,7 @@
 
     def z_copy(of, to):
         piece = gat.at[x, y, of, c]
-        return remote(piece, piece, z_ss.at[to], z_rs.at[of], at_z(to))
+        return remote(piece, piece, z_ss.at[0], z_rs.at[of], at_z(to))
 
     group = z // 4
     for off in (0, 3, 1, 2):
@@ -286,27 +290,17 @@
 
         def go(i):
             to = lax.rem(z + i, NZ)
-            remote(part.at[n, to], rsb.at[n, z], r_ss.at[n, i], r_rs.at[n, i], at_z(to)).start()
+            remote(part.at[n, to], rsb.at[n, z], r_ss.at[n], r_rs.at[n], at_z(to)).start()
 
         loop(1, NZ, go)
 
     def y_copy(n, i, slot):
         return remote(
-            ysend.at[n], yrec.at[n, slot], y_ss.at[n, i], y_rs.at[n, i], at_y(lax.rem(y + i, NY))
+            ysend.at[n], yrec.at[n, slot], y_ss.at[n], y_rs.at[n], at_y(lax.rem(y + i, NY))
         )
 
     def sum_middle(n):
-        def done(i):
-            to = lax.rem(z + i, NZ)
-            remote(
-                part.at[n, to],
-                rsb.at[n, lax.rem(z + NZ - i, NZ)],
-                r_ss.at[n, i],
-                r_rs.at[n, i],
-                at_z(to),
-            ).wait()
-
-        loop(1, NZ, done)
+        arrived(rsb.at[n, 0 : NZ - 1], r_rs.at[n])
         total = jnp.sum(rsb[n], axis=0)
         ysend[n] = total
         yrec[n, y] = total
@@ -314,15 +308,15 @@
 
     def g_copy(n, i, slot):
         piece = full.at[n, slot]
-        return remote(piece, piece, g_ss.at[n, i], g_rs.at[n, i], at_z(lax.rem(z + i, NZ)))
+        return remote(piece, piece, g_ss.at[n], g_rs.at[n], at_z(lax.rem(z + i, NZ)))
 
     def sum_last(n):
-        loop(1, NY, lambda i: y_copy(n, i, lax.rem(y + NY - i, NY)).wait())
+        arrived(yrec.at[n, 0 : NY - 1], y_rs.at[n])
         full[n, z] = jnp.sum(yrec[n], axis=0)
         loop(1, NZ, lambda i: g_copy(n, i, z).start())
 
     def sum_done(n):
-        loop(1, NZ, lambda i: g_copy(n, i, lax.rem(z + NZ - i, NZ)).wait())
+        arrived(full.at[n, 0 : NZ - 1], g_rs.at[n])
         return jnp.concatenate(
             [jnp.concatenate([full[n, 2 * k], full[n, 2 * k + 1]], axis=1) for k in range(8)], axis=0
         )
@@ -351,27 +345,23 @@
 
     def a1_copy(k, s, of, to):
         piece = gat.at[of, y, z_of(s, 0), c]
-        return remote(piece, piece, a1_ss.at[k, s], a1_rs.at[k, s], at_x(to))
+        return remote(piece, piece, n_ss.at[0], n_rs.at[(k + 1) // 2, s], at_x(to))
 
     def b1_copy(k, s, of, to):
         piece = gat.at[x, of, z_of(s, 1), c]
-        return remote(piece, piece, b1_ss.at[k, s], b1_rs.at[k, s], at_y(to))
+        return remote(piece, piece, n_ss.at[0], n_rs.at[(k + 1) // 2, s], at_y(to))
 
     def a2_copy(k, s, of, to):
         piece = gat.at[:, of, z_of(s, 0), c]
-        return remote(piece, piece, a2_ss.at[k, s], a2_rs.at[k, s], at_y(to))
+        return remote(piece, piece, w_ss.at[0], w_rs.at[(k + 1) // 2, s], at_y(to))
 
     def b2_copy(k, s, of, to):
         piece = gat.at[of, :, z_of(s, 1), c]
-        return remote(piece, piece, b2_ss.at[k, s], b2_rs.at[k, s], at_x(to))
-
-    def sa_copy(k, s, of, core):
-        piece = gat.at[:, of, z_of(s, 0), core]
-        return remote(piece, piece, s1_ss.at[k, s], s1_rs.at[k, s], sib)
-
-    def sb_copy(k, s, of, core):
-        piece = gat.at[of, :, z_of(s, 1), core]
-        return remote(piece, piece, s2_ss.at[k, s], s2_rs.at[k, s], sib)
+        return remote(piece, piece, w_ss.at[0], w_rs.at[(k + 1) // 2, s], at_x(to))
+
+    def core_copy(s):
+        piece = gat.at[:, :, pl.ds(z_of(s, 0), 2), c]
+        return remote(piece, piece, c_ss.at[0], c_rs.at[s], sib)
 
     def narrow_start(s):
         for k in range(2):
@@ -387,47 +377,28 @@
         b1_copy(1, s, y, behind_y).start()
 
     def narrow_pass(s):
-        a1_copy(0, s, behind_x, ahead_x).wait_recv()
+        arrived(pieces(2), n_rs.at[0, s])
         a1_copy(2, s, behind_x, ahead_x).start()
-        b1_copy(0, s, behind_y, ahead_y).wait_recv()
         b1_copy(2, s, behind_y, ahead_y).start()
 
     def wide_start(s):
-        a1_copy(1, s, ahead_x, behind_x).wait_recv()
-        a1_copy(2, s, far_x, ahead_x).wait_recv()
+        arrived(pieces(4), n_rs.at[1, s])
         a2_copy(0, s, y, ahead_y).start()
+        b2_copy(0, s, x, ahead_x).start()
         a2_copy(1, s, y, behind_y).start()
-        b1_copy(1, s, ahead_y, behind_y).wait_recv()
-        b1_copy(2, s, far_y, ahead_y).wait_recv()
-        b2_copy(0, s, x, ahead_x).start()
         b2_copy(1, s, x, behind_x).start()
-        sa_copy(0, s, y, c).start()
-        sb_copy(0, s, x, c).start()
 
     def wide_pass(s):
-        a2_copy(0, s, behind_y, ahead_y).wait_recv()
+        arrived(pieces(8), w_rs.at[0, s])
         a2_copy(2, s, behind_y, ahead_y).start()
-        b2_copy(0, s, behind_x, ahead_x).wait_recv()
         b2_copy(2, s, behind_x, ahead_x).start()
-        sa_copy(1, s, behind_y, c).start()
-        sb_copy(1, s, behind_x, c).start()
-        a2_copy(1, s, ahead_y, behind_y).wait_recv()
-        sa_copy(2, s, ahead_y, c).start()
-        b2_copy(1, s, ahead_x, behind_x).wait_recv()
-        sb_copy(2, s, ahead_x, c).start()
 
     def wide_end(s):
-        a2_copy(2, s, far_y, ahead_y).wait_recv()
-        sa_copy(3, s, far_y, c).start()
-        b2_copy(2, s, far_x, ahead_x).wait_recv()
-        sb_copy(3, s, far_x, c).start()
+        arrived(pieces(16), w_rs.at[1, s])
+        core_copy(s).start()
 
     def core_end(s):
-        for k, (fy, fx) in enumerate(
-            ((y, x), (ahead_y, ahead_x), (behind_y, behind_x), (far_y, far_x))
-        ):
-            sa_copy(k, s, fy, 1 - c).wait()
-            sb_copy(k, s, fx, 1 - c).wait()
+        core_copy(s).wait_recv()
 
     def project(s):
         g = group_of(s)
@@ -458,7 +429,7 @@
         at_tick(t, 6, wide_pass)
         at_tick(t, 8, wide_end)
         at_tick(t, 9, core_end)
-        at_tick(t, 0, lambda s: loop(6 * s, 6 * s + 6, flip))
+        at_tick(t, 0, lambda s: loop(24 + 3 * s, 24 + 3 * s + 3, flip))
 
         @pl.when((t >= 9) & (lax.rem(t, 2) == 0))
         def _():
@@ -532,22 +503,22 @@
 
     def xo_copy(s):
         return remote(
-            yb.at[far_x, :, piece_z(s, 0, c)], axo.at[s], p1_ss.at[0, s], p1_rs.at[0, s], at_x(ahead_x)
+            yb.at[far_x, :, piece_z(s, 0, c)], axo.at[s], p1_ss.at[0], p1_rs.at[0, s], at_x(ahead_x)
         )
 
     def yo_copy(s):
         return remote(
-            yb.at[:, far_y, piece_z(s, 1, c)], byo.at[s], p1_ss.at[1, s], p1_rs.at[1, s], at_y(ahead_y)
+            yb.at[:, far_y, piece_z(s, 1, c)], byo.at[s], p1_ss.at[0], p1_rs.at[1, s], at_y(ahead_y)
         )
 
     def xr_copy(k, s, to):
         return remote(
-            yb.at[to, :, piece_z(s, 0, c)], axr.at[k, s], p1_ss.at[2 + k, s], p1_rs.at[2 + k, s], at_x(to)
+            yb.at[to, :, piece_z(s, 0, c)], axr.at[k, s], p1_ss.at[0], p1_rs.at[2, s], at_x(to)
         )
 
     def yr_copy(k, s, to):
         return remote(
-            yb.at[:, to, piece_z(s, 1, c)], byr.at[k, s], p1_ss.at[4 + k, s], p1_rs.at[4 + k, s], at_y(to)
+            yb.at[:, to, piece_z(s, 1, c)], byr.at[k, s], p1_ss.at[0], p1_rs.at[3, s], at_y(to)
         )
 
     def add_core(s):
@@ -576,22 +547,20 @@
 
     def qy_copy(s, i):
         to = lax.rem(y + i, NY)
-        return remote(ya.at[s, to], ayb.at[s, i], p2_ss.at[0, s, i], p2_rs.at[0, s, i], at_y(to))
+        return remote(ya.at[s, to], ayb.at[s, i], p2_ss.at[0], p2_rs.at[0, s], at_y(to))
 
     def qx_copy(s, i):
         to = lax.rem(x + i, NX)
-        return remote(yc.at[s, to], bxb.at[s, i], p2_ss.at[1, s, i], p2_rs.at[1, s, i], at_x(to))
+        return remote(yc.at[s, to], bxb.at[s, i], p2_ss.at[0], p2_rs.at[1, s], at_x(to))
 
     def add_first(s):
-        xr_copy(0, s, ahead_x).wait_recv()
-        xr_copy(1, s, behind_x).wait_recv()
+        arrived(pieces(8), p1_rs.at[2, s])
         ya[s] = (
             yb[x, :, piece_z(s, 0, c)].astype(F32) + axr[0, s].astype(F32) + axr[1, s].astype(F32)
         ).astype(BF16)
         for i in (2, 1, 3):
             qy_copy(s, i).start()
-        yr_copy(0, s, ahead_y).wait_recv()
-        yr_copy(1, s, behind_y).wait_recv()
+        arrived(pieces(8), p1_rs.at[3, s])
         yc[s] = (
             yb[:, y, piece_z(s, 1, c)].astype(F32) + byr[0, s].astype(F32) + byr[1, s].astype(F32)
         ).astype(BF16)
@@ -600,15 +569,11 @@
 
     def t_copy(s, k):
         to = piece_z(s, k, c)
-        return remote(zsend.at[s, k], zr.at[z], p3_ss.at[2 * s + k], p3_rs.at[z], at_z(to))
+        return remote(zsend.at[s, k], zr.at[z], p3_ss.at[0], p3_rs.at[0], at_z(to))
 
     def add_second(s):
         for k in range(2):
-            for i in (1, 3, 2):
-                if k == 0:
-                    qy_copy(s, i).wait()
-                else:
-                    qx_copy(s, i).wait()
+            arrived(pieces(3), p2_rs.at[k, s])
             piece = (ya[s, y] if k == 0 else yc[s, x]).astype(F32)
             for i in (1, 2, 3):
                 piece = piece + (ayb[s, i] if k == 0 else bxb[s, i]).astype(F32)
@@ -663,7 +628,7 @@
 
     def h_copy(i, slot):
         to = lax.rem(e + i, 8)
-        return remote(asend.at[to], afin.at[slot], h_ss.at[i], h_rs.at[i], (to, j))
+        return remote(asend.at[to], afin.at[slot], h_ss.at[0], h_rs.at[0], (to, j))
 
     loop(1, 8, lambda i: h_copy(i, e).start())
     first = SCALE * dot_nt(r13, xj[...])
@@ -679,11 +644,7 @@
 
     @pl.when(holder)
     def _():
-        def got(i):
-            of = lax.rem(z + i, NZ)
-            remote(zsend.at[0, 0], zr.at[of], p3_ss.at[0], p3_rs.at[of], at_z(of)).wait_recv()
-
-        loop(1, NZ, got)
+        arrived(pieces(NZ - 1), p3_rs.at[0])
         fscr[...] = jnp.zeros_like(fscr)
         fscr[pl.ds(pl.multiple_of(HR * rh, HR), HR), :] = jnp.sum(zr[...].astype(F32), axis=0)
         fsend[...] = jnp.transpose(fscr[...]).astype(BF16).reshape(4, TB, 128)
@@ -697,7 +658,7 @@
             def _():
                 f_copy(i).start()
 
-    loop(1, 8, lambda i: h_copy(i, lax.rem(e + 8 - i, 8)).wait())
+    arrived(afin.at[0:7], h_rs.at[0])
 
     total = jnp.zeros((TB, 128), F32)
     first_k = jnp.zeros((TB, 1), F32)
@@ -729,32 +690,26 @@
             def _():
                 f_copy(i).wait_send()
 
-    def z_sent(i):
-        z_copy(z, lax.rem(z + i, NZ)).wait_send()
-
-    loop(1, NZ, z_sent)
-
-    def gather_sent(s):
-        for k in range(3):
-            a1_copy(k, s, x, ahead_x).wait_send()
-            b1_copy(k, s, y, ahead_y).wait_send()
-            a2_copy(k, s, y, ahead_y).wait_send()
-            b2_copy(k, s, x, ahead_x).wait_send()
-
-    loop(0, 8, gather_sent)
-
-    def scatter_sent(s):
-        xo_copy(s).wait_send()
-        yo_copy(s).wait_send()
-        for k in range(2):
-            xr_copy(k, s, ahead_x).wait_send()
-            yr_copy(k, s, ahead_y).wait_send()
-
-            @pl.when(piece_z(s, k, c) != z)
-            def _():
-                t_copy(s, k).wait_send()
-
-    loop(0, 4, scatter_sent)
+    left(disp.at[0:7], d_ss.at[0])
+    left(pieces(NZ - 1), z_ss.at[0])
+    left(gat.at[0, :, 0:6], n_ss.at[0])
+    left(gat.at[:, :, 0:6], w_ss.at[0])
+    left(gat.at[:, :, :, 0], c_ss.at[0])
+    for n in range(2):
+        left(rsb.at[n, 0 : NZ - 1], r_ss.at[n])
+        left(yrec.at[n, 0 : NY - 1], y_ss.at[n])
+        left(full.at[n, 0 : NZ - 1], g_ss.at[n])
+    left(yb.at[:, :, 0:6], p1_ss.at[0])
+    left(gat.at[0, 0:2, 0:12, 0], p2_ss.at[0])
+    left(afin.at[0:7], h_ss.at[0])
+
+    @pl.when(holder)
+    def _():
+        left(pieces(7), p3_ss.at[0])
+
+    @pl.when(jnp.logical_not(holder))
+    def _():
+        left(pieces(8), p3_ss.at[0])
 
 
 def finish(*refs):
@@ -852,40 +807,34 @@
             buf((8, TB, 128)),
             buf((8, TB, 128)),
             dma((13,)),
+            dma((1,)),
+            dma((1,)),
+            dma((1,)),
+            dma((NZ,)),
+            dma((1,)),
+            dma((2, 8)),
+            dma((1,)),
+            dma((2, 8)),
+            dma((1,)),
             dma((8,)),
-            dma((8,)),
-            dma((NZ,)),
-            dma((NZ,)),
-            dma((3, 8)),
-            dma((3, 8)),
-            dma((3, 8)),
-            dma((3, 8)),
-            dma((3, 8)),
-            dma((3, 8)),
-            dma((3, 8)),
-            dma((3, 8)),
-            dma((4, 8)),
-            dma((4, 8)),
-            dma((4, 8)),
-            dma((4, 8)),
-            dma((2, NZ)),
-            dma((2, NZ)),
-            dma((2, NY)),
-            dma((2, NY)),
-            dma((2, NZ)),
-            dma((2, NZ)),
+            dma((2,)),
+            dma((2,)),
+            dma((2,)),
+            dma((2,)),
+            dma((2,)),
+            dma((2,)),
             dma((4,)),
             dma((4,)),
-            dma((6, 4)),
-            dma((6, 4)),
-            dma((2, 4, 4)),
-            dma((2, 4, 4)),
-            dma((8,)),
-            dma((NZ,)),
+            dma((1,)),
+            dma((4, 4)),
+            dma((1,)),
+            dma((2, 4)),
+            dma((1,)),
+            dma((1,)),
             dma((4,)),
             dma((2,)),
-            dma((8,)),
-            dma((8,)),
+            dma((1,)),
+            dma((1,)),
             pltpu.SemaphoreType.REGULAR,
         ],
         compiler_params=pltpu.CompilerParams(

time: 98.9 us -> 93.6 us (0.946)
  Pallas kernels: 98.1 us -> 92.9 us
    pallas_call x1, Pallas kernels: 95.2 us -> 89.9 us  [local(): pl.pallas_call(kernel, out_shape=(jax.ShapeDtypeStruct((TB, FD), BF16), j...]
where the time goes in v3:
time: 93.6 us; the launch traced here: 93.5 us
  Pallas kernels  92.9 us (99%)
    pallas_call x1, Pallas kernels, local(): pl.pallas_call(kernel, out_shape=(jax.ShapeDtypeStruct((TB, FD), BF16), j...  89.9 us
    pallas_call x1, Pallas kernels, local(): pl.pallas_call(finish, out_shape=[jax.ShapeDtypeStruct(o.shape, o.dtype)...  2.95 us

profile of v3, /device:TPU:1, one launch (start us, length us, event | category | flops | bytes accessed | tf_op | source)
XLA Modules:
  0.0 93.5 jit_solution(14959048915123673584)
XLA Ops:
  0.6 89.9 %moe_backward.1 = (bf16[32,96]{1,0:T(8,128)(2,1)}, f32[2,32]{1,0:T(2,128)}, f32[1,16,96]{2,1,0:T(8,128)}, f32[1,16,128]{2,1,0:T(8,128)}, f32[1,16,96]{2,1,0:T(8,...) custom-call(bf16[32,96]{1,0:T(8,128)(2,1)} %tok_hbm.1, bf16[32,96]{1,0:T(8,128)(2,1)} %ups_hbm.1, ...), custom_call_target="tpu_custom_call" | custom-call | tf_op jit(solution)/shard_map/moe_backward/pallas_call | solution.py:747
  90.6 2.9 %hand_over.1 = (bf16[32,96]{1,0:T(8,128)(2,1)}, f32[2,32]{1,0:T(2,128)}, f32[1,16,96]{2,1,0:T(8,128)}, f32[1,16,128]{2,1,0:T(8,128)}, f32[1,16,96]{2,1,0:T(8,128...) custom-call(bf16[32,96]{1,0:T(8,128)(2,1)} %get-tuple-element.24.refs_0_, ...), custom_call_target="tpu_custom_call" | custom-call | tf_op jit(solution)/shard_map/hand_over/pallas_call | solution.py:859

commit v4 on v3

--- a/solution.py
+++ b/solution.py
@@ -595,26 +595,26 @@
 
     def scatter_tick(t):
         at_step(t, 0, grads)
-        at_step(t, 4, add_second)
-        at_step(t, 3, add_first)
-        at_step(t, 2, add_far)
         at_step(t, 1, add_core)
-
-        @pl.when(t == 3)
+        at_step(t, 3, add_far)
+        at_step(t, 5, add_first)
+        at_step(t, 7, add_second)
+
+        @pl.when(t == 5)
         def _():
             sum_middle(1)
 
-        @pl.when(t == 4)
+        @pl.when(t == 9)
         def _():
             dft[0] = SCALE * dot_nt((weight * v).astype(BF16), hidden)
             gs[0] = SCALE * dot_nt(u1, e1)
             us[0] = SCALE * dot_nt(u3, e3)
 
-        @pl.when(t == 5)
+        @pl.when(t == 7)
         def _():
             sum_last(1)
 
-    loop(0, 8, scatter_tick)
+    loop(0, 11, scatter_tick)
 
     holder = lax.rem(z, 4) // 2 == c
     sums = sum_done(1)

time: 93.6 us -> 89.8 us (0.959)
  Pallas kernels: 92.9 us -> 89 us
    pallas_call x1, Pallas kernels: 89.9 us -> 86.1 us  [local(): pl.pallas_call(kernel, out_shape=(jax.ShapeDtypeStruct((TB, FD), BF16), j...]
where the time goes in v4:
time: 89.8 us; the launch traced here: 89.7 us
  Pallas kernels  89 us (99%)
    pallas_call x1, Pallas kernels, local(): pl.pallas_call(kernel, out_shape=(jax.ShapeDtypeStruct((TB, FD), BF16), j...  86.1 us
    pallas_call x1, Pallas kernels, local(): pl.pallas_call(finish, out_shape=[jax.ShapeDtypeStruct(o.shape, o.dtype)...  2.95 us

profile of v4, /device:TPU:1, one launch (start us, length us, event | category | flops | bytes accessed | tf_op | source)
XLA Modules:
  0.0 89.7 jit_solution(6391764443555373994)
XLA Ops:
  0.6 86.1 %moe_backward.1 = (bf16[32,96]{1,0:T(8,128)(2,1)}, f32[2,32]{1,0:T(2,128)}, f32[1,16,96]{2,1,0:T(8,128)}, f32[1,16,128]{2,1,0:T(8,128)}, f32[1,16,96]{2,1,0:T(8,...) custom-call(bf16[32,96]{1,0:T(8,128)(2,1)} %tok_hbm.1, bf16[32,96]{1,0:T(8,128)(2,1)} %ups_hbm.1, ...), custom_call_target="tpu_custom_call" | custom-call | tf_op jit(solution)/shard_map/moe_backward/pallas_call | solution.py:747
  86.7 2.9 %hand_over.1 = (bf16[32,96]{1,0:T(8,128)(2,1)}, f32[2,32]{1,0:T(2,128)}, f32[1,16,96]{2,1,0:T(8,128)}, f32[1,16,128]{2,1,0:T(8,128)}, f32[1,16,96]{2,1,0:T(8,128...) custom-call(bf16[32,96]{1,0:T(8,128)(2,1)} %get-tuple-element.24.refs_0_, ...), custom_call_target="tpu_custom_call" | custom-call | tf_op jit(solution)/shard_map/hand_over/pallas_call | solution.py:859
